TPU v7x, 256 devices: a whole 4x4x8 slice. The times are simulated.
256 devices in a mesh: frame: 4 (over y_lo, core), slab: 64 (over x, y_hi, z).
Axes of the slice: x: 4, y: 4 (y_hi: 2, y_lo: 2; y = y_hi * 2 + y_lo), z: 8, core: 2. Of those that a mesh axis runs over, the one named last changes fastest.
Arguments:
- element_data: bfloat16 [1024, 4, 4096], P('slab', 'frame'), may hold values from -6 to 6
- migration: bfloat16 [2048, 1024], replicated, may hold values from -0.1875 to 0.1875
- column_gain: float32 [2048], replicated, may hold values from 0.3 to 3
- depth_gain: float32 [4096], P('slab'), may hold values from 0.3 to 3
- coarse_shift: int32 [3, 4, 4, 8, 256], P(None, 'frame', None, None, 'slab'), may hold values from -8 to 8
- reference_frame: int32 [4], replicated, may hold values from 0 to 3, each once
Outputs:
- scores: float32 [7, 4, 4, 8, 256], P(None, 'frame', None, None, 'slab')
- displacement: float32 [3, 4, 4, 8, 256], P(None, 'frame', None, None, 'slab')
Inputs may be any that keep to these rules, and one draw needn't show every extreme that they name: `reference_frame`: each frame index appears exactly once; the first entry names the reference frame, which serves all blocks.
All inputs are finite; a program needn't handle non-finite values.
Results may differ from a plain program's by a relative error of at most 0.0039.
Values may be sent and summed in bfloat16 or wider, within the bound.
A program may use at most 64 MiB of HBM per device.

v0:
```python
import math

import jax
import jax.numpy as jnp
from jax import lax
from jax.sharding import PartitionSpec as P

LX = 32
LY = 64
KX = 8
KY = 8
KZ = 16
CMAX = 8


epsilon = 1e-05
shift_table = ((0, 0, 0), (-1, 0, 0), (1, 0, 0), (0, -1, 0), (0, 1, 0), (0, 0, -1), (0, 0, 1))


def spread(value, axis, source):
    kept = jnp.where(lax.axis_index(axis) == source, value, 0).astype(value.dtype)
    return lax.psum(kept, axis)


def padded_2(array, sides, width):
    for axis, dim in sides:
        devices, length = (lax.axis_size(axis), array.shape[dim])
        up = [(i, (i + 1) % devices) for i in range(devices - 1)]
        down = [(j, i) for i, j in up]
        last = lax.slice_in_dim(array, length - width, length, axis=dim)
        initial = lax.slice_in_dim(array, 0, width, axis=dim)
        before = lax.ppermute(last, axis, up)
        after = lax.ppermute(initial, axis, down)
        array = jnp.concatenate([before, array, after], axis=dim)
    return array


def migrate(pieces, migration, column_gain, depth_gain):
    elements, items, depth_count = pieces.shape
    flattened = pieces.reshape(elements, items * depth_count)
    raw_image = jnp.dot(migration, flattened, preferred_element_type=jnp.float32)
    raw_image = raw_image.reshape(migration.shape[0], items, depth_count)
    scaled = raw_image * column_gain[:, None, None] * depth_gain[None, None, :]
    return scaled.astype(jnp.bfloat16)


def block_scores(kernels, padded, starts):
    kernel_shape = kernels.shape[1:]
    box_shape = (kernel_shape[0] + 2, kernel_shape[1] + 2, kernel_shape[2] + 2)

    def take_box(first, second, third):
        return lax.dynamic_slice(padded, (first - 1, second - 1, third - 1), box_shape)

    boxes = jax.vmap(take_box)(starts[0], starts[1], starts[2])
    cell_count = kernel_shape[0] * kernel_shape[1] * kernel_shape[2]
    kernel_float = kernels.astype(jnp.float32)
    kernel_power = jnp.mean(kernel_float * kernel_float, axis=(1, 2, 3))
    results = []
    for shift_step in shift_table:
        low = [1 + shift_step[dimension] for dimension in range(3)]
        window = boxes[
            :,
            low[0] : low[0] + kernel_shape[0],
            low[1] : low[1] + kernel_shape[1],
            low[2] : low[2] + kernel_shape[2],
        ].astype(jnp.float32)
        cross_mean = jnp.mean(kernel_float * window, axis=(1, 2, 3))
        window_power = jnp.mean(window * window, axis=(1, 2, 3))
        results.append(
            math.sqrt(cell_count)
            * cross_mean
            / jnp.sqrt((kernel_power + epsilon) * (window_power + epsilon))
        )
    return jnp.stack(results)


def refine(scores, shifts):
    refined = []
    for dimension in range(3):
        lower_score = scores[1 + 2 * dimension]
        upper_score = scores[2 + 2 * dimension]
        curvature = jnp.maximum(2.0 * scores[0] - lower_score - upper_score, 1.0)
        refined.append(
            shifts[dimension].astype(jnp.float32) + (upper_score - lower_score) / (2.0 * curvature)
        )
    return jnp.stack(refined)


def per_device(element_data, migration, column_gain, depth_gain, coarse_shift, reference_frame):
    frames_here = element_data.shape[1]
    depth_here = depth_gain.shape[0]
    margin = CMAX + 1
    chosen = reference_frame[0]
    owner_index = chosen // frames_here
    position = chosen % frames_here
    images = migrate(
        lax.all_to_all(element_data, "slab", split_axis=2, concat_axis=0, tiled=True),
        migration,
        column_gain,
        depth_gain,
    )
    candidate = lax.dynamic_index_in_dim(images, position, 1, keepdims=False)
    volume = spread(candidate, "frame", owner_index)
    lattice = volume.reshape(LX, LY, depth_here)
    extended = padded_2(lattice, (("slab", 2),), margin)
    padded = jnp.pad(extended, ((margin, margin), (margin, margin), (0, 0)))
    kernel_shape = (KX, KY, KZ)
    block_counts = (LX // KX, LY // KY, depth_here // KZ)
    arranged = images.reshape(
        block_counts[0], KX, block_counts[1], KY, frames_here, block_counts[2], KZ
    )
    kernels = arranged.transpose(4, 0, 2, 5, 1, 3, 6).reshape(frames_here, -1, KX, KY, KZ)
    layout = (frames_here, block_counts[0], block_counts[1], block_counts[2])
    block_index = [
        lax.broadcasted_iota(jnp.int32, layout, dimension + 1).reshape(frames_here, -1)
        for dimension in range(3)
    ]
    shifts = coarse_shift.reshape(3, frames_here, -1)
    starts = jnp.stack(
        [
            block_index[dimension] * kernel_shape[dimension] + shifts[dimension] + margin
            for dimension in range(3)
        ]
    )
    frame_starts = starts.transpose(1, 0, 2)

    def per_frame(inputs):
        frame_kernels, frame_start = inputs
        return block_scores(frame_kernels, padded, [frame_start[0], frame_start[1], frame_start[2]])

    framed = lax.map(per_frame, (kernels, frame_starts))
    scores = framed.transpose(1, 0, 2).reshape(7, -1)
    displacement = refine(scores, shifts.reshape(3, -1))
    return (scores.reshape((7,) + layout), displacement.reshape((3,) + layout))


def solution(mesh):
    placed = (
        P("slab", "frame", None),
        P(),
        P(),
        P("slab"),
        P(None, "frame", None, None, "slab"),
        P(),
    )
    return jax.shard_map(
        per_device,
        mesh=mesh,
        in_specs=placed,
        out_specs=(P(None, "frame", None, None, "slab"), P(None, "frame", None, None, "slab")),
        check_vma=False,
    )
```

profile of v0, /device:TPU:1, one launch (start us, length us, event | category | flops | bytes accessed | tf_op | source)
XLA Modules:
  0.0 589.3 jit_solution(7783451355229198082)
XLA Ops:
  7.2 4.3 copy.74
  12.0 22.4 %reduce.3 = bf16[4096,16]{1,0:T(8,128)(2,1)S(1)} reduce(bf16[4096,1,16]{2,1,0:T(2,128)(2,1)S(1)} %bitcast.47, bf16[]{:T(256)} %broadcast.790), dimensions={1}, to_apply=%bitcast.33.reduce_sub_computation | reduce | bytes 262146
  36.2 15.1 %all-to-all-start = ((bf16[64,2,512]{2,1,0:T(2,128)(2,1)}), bf16[64,2,512]{2,1,0:T(2,128)(2,1)S(1)}, u32[]{:S(2)}, u32[]{:S(2)}) async-start(bf16[64,2,512]{2,1,0:T(2,128)(2,1)} %reshape.756), calls=%async_computation | async-start | bytes 262144 | tf_op jit(solution)/shard_map/all_to_all | solution.py:97
  52.7 10.2 %all-to-all-done = bf16[64,2,512]{2,1,0:T(2,128)(2,1)S(1)} async-done(((bf16[64,2,512]{2,1,0:T(2,128)(2,1)}), bf16[64,2,512]{2,1,0:T(2,128)(2,1)S(1)}, u32[]{:S(2)}, u32[]{:S(2)}) %all-to-all-start) | async-done | bytes 131104 | tf_op jit(solution)/shard_map/all_to_all | solution.py:97
  67.1 3.6 broadcast_select_fusion
  72.1 3.3 mul.491
  75.4 3.2 reduce_sum.151
  78.5 30.6 %all-reduce.3.cloned.1.call-done = bf16[32,64,64]{2,1,0:T(8,128)(2,1)} async-done(((bf16[32,64,64]{2,1,0:T(8,128)(2,1)}), bf16[32,64,64]{2,1,0:T(8,128)(2,1)}) %all-reduce.3.cloned.1.call-update) | async-done | bytes 262160 | tf_op jit(solution)/shard_map/psum | solution.py:22
  111.5 3.2 collective-permute-start
  116.2 3.3 reshape.755
  119.5 4.9 copy.78
  126.1 3.5 collective-permute-done.1
  130.5 425.3 %while.1 = (s32[]{:T(128)}, bf16[50,82,82]{2,1,0:T(8,128)(2,1)S(1)}, s32[128,3]{0,1:T(4,128)S(1)}, bf16[128,10,10,18]{3,2,1,0:T(8,128)(2,1)}, s32[]{:T(128)}) while((s32[]{:T(128)}, bf16[50,82,82]{2,1,0:T(8,128)(2,1)S(1)}, s32[128,3]{0,1:T(4,128)S(1)}, bf16[128,10,10,18]{3,2,1,0:T(8,128)(2,1)}, s32[]{:T(128)}) %tuple.58), condition=%wide.while_cond, body=%wide.while_body.sunk | while | flops 2 | bytes 46721 | solution.py:52
  164.4 2.7 bitcast_dynamic-update-slice_fusion.2
  304.0 2.7 bitcast_dynamic-update-slice_fusion.2
  327.2 2.7 bitcast_dynamic-update-slice_fusion.2
  360.5 2.7 bitcast_dynamic-update-slice_fusion.2
  430.2 2.7 bitcast_dynamic-update-slice_fusion.2
  473.4 2.7 bitcast_dynamic-update-slice_fusion.2
  506.7 2.7 bitcast_dynamic-update-slice_fusion.2
  516.6 2.7 bitcast_dynamic-update-slice_fusion.2
  533.2 2.7 bitcast_dynamic-update-slice_fusion.2
  546.5 2.7 bitcast_dynamic-update-slice_fusion.2
  555.8 23.2 %fusion.13 = (f32[128]{0:T(128)S(1)}, f32[128]{0:T(128)S(1)}, f32[128]{0:T(128)S(1)}, f32[128]{0:T(128)S(1)}, f32[128]{0:T(128)S(1)}, /*index=5*/f32[128]{0:T(12...) fusion(bf16[128,10,10,18]{3,2,1,0:T(8,128)(2,1)} %get-tuple-ele, ...), kind=kLoop, calls=%fused_computation.29 | loop fusion | flops 4585728 | bytes 2366464 | tf_op jit(solution)/shard_map/while/body/eval_jaxpr/reduce_sum | solution.py:68
  (459 shorter events, 417.1 us)
Async XLA Ops:
  7.2 44.5 %copy-start.1 = (s32[3,1,4,8,4]{3,4,2,1,0:T(4,128)S(1)}, s32[3,1,4,8,4]{3,4,2,1,0:T(4,128)}, u32[]{:S(2)}) copy-start(s32[3,1,4,8,4]{3,4,2,1,0:T(4,128)} %param.10) | copy-start | bytes 4612
  7.2 45.4 %copy-start.4 = (s32[4]{0:T(128)S(1)}, s32[4]{0:T(128)}, u32[]{:S(2)}) copy-start(s32[4]{0:T(128)} %param.11) | copy-start | bytes 52
  34.4 32.7 %copy-start.2 = (f32[2048]{0:T(1024)S(1)}, f32[2048]{0:T(1024)}, u32[]{:S(2)}) copy-start(f32[2048]{0:T(1024)} %param.8) | copy-start | bytes 24580
  34.5 32.7 %copy-start.3 = (f32[64]{0:T(128)S(1)}, f32[64]{0:T(128)}, u32[]{:S(2)}) copy-start(f32[64]{0:T(128)} %param.9) | copy-start | bytes 772
  36.2 26.6 %all-to-all-start = ((bf16[64,2,512]{2,1,0:T(2,128)(2,1)}), bf16[64,2,512]{2,1,0:T(2,128)(2,1)S(1)}, u32[]{:S(2)}, u32[]{:S(2)}) async-start(bf16[64,2,512]{2,1,0:T(2,128)(2,1)} %reshape.756), calls=%async_computation | async-start | bytes 262144 | tf_op jit(solution)/shard_map/all_to_all | solution.py:97
  51.4 57.8 %all-reduce.3.cloned.1.call-start = ((), (), s32[]{:S(2)}) async-start(), calls=%async_computation.1 | async-start | bytes 1048576 | tf_op jit(solution)/shard_map/psum | solution.py:22
  111.5 14.6 %collective-permute-start = (bf16[32,64,9]{2,1,0:T(8,128)(2,1)}, bf16[32,64,9]{2,1,0:T(8,128)(2,1)S(1)}, u32[]{:S(2)}, u32[]{:S(2)}) collective-permute-start(bf16[32,64,9]{2,1,0:T(8,128)(2,1)} %get-tuple-element.69), channel_id=1, source_target_pairs={{0,1},{1,2},{2,3},{3,4},{4,5},{5,6},{6,7},{7,8},{8,9},{9,10},{10,1... | collective-permute-start | bytes 110600 | tf_op jit(solution)/shard_map/ppermute | solution.py:32
  114.7 14.9 %collective-permute-start.1 = (bf16[32,64,9]{2,1,0:T(8,128)(2,1)S(1)}, bf16[32,64,9]{2,1,0:T(8,128)(2,1)S(1)}, u32[]{:S(2)}, u32[]{:S(2)}) collective-permute-start(bf16[32,64,9]{2,1,0:T(8,128)(2,1)S(1)} %get-tuple-element.70), channel_id=1, source_target_pairs={{1,0},{2,1},{3,2},{4,3},{5,4},{6,5},{7,6},{8,7},{9,8},{10,9},{11,1... | collective-permute-start | bytes 110600 | tf_op jit(solution)/shard_map/ppermute | solution.py:33
  119.5 10.1 %copy-start = (bf16[32,64,64]{2,1,0:T(8,128)(2,1)S(1)}, bf16[32,64,64]{2,1,0:T(8,128)(2,1)}, u32[]{:S(2)}) copy-start(bf16[32,64,64]{2,1,0:T(8,128)(2,1)} %all-reduce.3.cloned.1.call-done) | copy-start | bytes 786436
Sparse Core Ops, SparseCore 0:
  71.9 37.2 all-reduce.2
where the time goes:
time: 596 us; the launch traced here: 589 us
  local copies, waits for them, and re-layouts  455 us (76%)
  other arithmetic  50 us (8%)
  waiting for transfers between devices  45.9 us (8%)
  starting transfers between devices  19.8 us (3%)
  between operations  14.6 us (2%)
    gather x384, local copies, waits for them, and re-layouts  425 us
    psum x1, waiting for transfers between devices, spread(): return lax.psum(kept, axis)  30.6 us
    reduce_sum x1, other arithmetic, block_scores(): window_power = jnp.mean(window * window, axis=(1, 2, 3))  23.2 us
    unnamed x6, other arithmetic  22.5 us
    all_to_all x1, starting transfers between devices, per_device(): lax.all_to_all(element_data, 'slab', split_axis=2, concat_axis=0, tiled=T...  15.1 us
  transfers between devices with their start and end apart: 4, of which 4 were waited for; matrix products, arithmetic and copies ran while one was open for 3% of the time, Pallas kernels for 0%

commit v1 on v0

v1 whole, which is shorter than its diff:
```python
import functools

import jax
import jax.numpy as jnp
from jax import lax
from jax.experimental import pallas as pl
from jax.experimental.pallas import tpu as pltpu
from jax.sharding import PartitionSpec as P

LX, LY = 32, 64
KX, KY, KZ = 8, 8, 16
MARGIN = 9
YPAD = 16
GROUP = 32
BLOCKS = 4
EPS = 1e-5
CELLS = KX * KY * KZ
ROWS = 256


def expand_gain(gain_ref, wide_ref):
    for i in range(gain_ref.shape[0]):
        row = jnp.broadcast_to(gain_ref[i : i + 1, :], (128, 128))
        wide_ref[pl.ds(i * 128, 128), :] = jnp.transpose(row)


def clear(volume_ref):
    def one(i, carry):
        volume_ref[i] = jnp.zeros(volume_ref.shape[1:], volume_ref.dtype)
        return carry

    lax.fori_loop(0, volume_ref.shape[0], one, 0)


def make_images(migration_ref, samples_ref, gain_ref, depth_ref, image_ref, volume_ref):
    planes = ROWS // LY

    def one(i, carry):
        rows = pl.ds(pl.multiple_of(i * ROWS, ROWS), ROWS)
        raw = jnp.dot(migration_ref[rows, :], samples_ref[...], preferred_element_type=jnp.float32)
        gain = gain_ref[rows, :]
        own = (raw[:, :128] * gain * depth_ref[0:1, :]).astype(jnp.bfloat16)
        image_ref[rows, :] = own.astype(jnp.float32)
        ref = (raw[:, 128:] * gain * depth_ref[1:2, :]).astype(jnp.bfloat16)
        ref = ref.astype(jnp.float32)
        for j in range(planes):
            volume_ref[MARGIN + i * planes + j, YPAD : YPAD + LY, :] = ref[j * LY : (j + 1) * LY]
        return carry

    lax.fori_loop(0, LX * LY // ROWS, one, 0)


def correlate(image_ref, volume_ref, shift_ref, parts_ref):
    lane = lax.broadcasted_iota(jnp.int32, (8, 128), 1)
    inside = lane % GROUP
    first = lane < GROUP
    third = lane < 3 * GROUP
    half = lane < 2 * GROUP
    center_mask = (inside >= 1) & (inside < 1 + KZ)
    before_mask = inside < KZ
    after_mask = (inside >= 2) & (inside < 2 + KZ)

    def one(g, carry):
        bx = g // 8
        by = g % 8
        xs, ys, turns = [], [], []
        for b in range(BLOCKS):
            xs.append(bx * KX + shift_ref[0, bx, b, by] + MARGIN)
            ys.append(by * KY + shift_ref[1, bx, b, by] + YPAD)
            turns.append((GROUP * b + 1 - MARGIN - KZ * b + 128 - shift_ref[2, bx, b, by]) % 128)

        def aligned(p, q):
            turned = [
                pltpu.roll(volume_ref[xs[b] + p, pl.ds(ys[b] + q, 8), :], turns[b], 1)
                for b in range(BLOCKS)
            ]
            return jnp.where(
                half,
                jnp.where(first, turned[0], turned[1]),
                jnp.where(third, turned[2], turned[3]),
            )

        def kernel_plane(p):
            row = pl.multiple_of((bx * KX + p) * LY + by * KY, 8)
            return image_ref[pl.ds(row, 8), :]

        zero = jnp.zeros((8, 128), jnp.float32)
        cross = [zero] * 7
        core, xm, xp, ym, yp, own = zero, zero, zero, zero, zero, zero
        for p in range(-1, KX + 1):
            window = aligned(p, 0)
            power = window * window
            if 0 <= p < KX:
                kernel = kernel_plane(p)
                own = own + kernel * kernel
                cross[0] += kernel * window
                cross[5] += pltpu.roll(kernel, 127, 1) * window
                cross[6] += pltpu.roll(kernel, 1, 1) * window
                low, high = aligned(p, -1), aligned(p, 1)
                cross[3] += kernel * low
                cross[4] += kernel * high
                ym = ym + low * low
                yp = yp + high * high
                core = core + power
            if p < KX - 1:
                cross[1] += kernel_plane(p + 1) * window
                xm = xm + power
            if p > 0:
                cross[2] += kernel_plane(p - 1) * window
                xp = xp + power
        slots = cross + [own]
        for value, mask in (
            (core, center_mask),
            (xm, center_mask),
            (xp, center_mask),
            (ym, center_mask),
            (yp, center_mask),
            (core, before_mask),
            (core, after_mask),
        ):
            slots.append(jnp.where(mask, value, 0.0))
        slots.append(own)
        for k, value in enumerate(slots):
            parts_ref[pl.ds(pl.multiple_of(k * 256 + g * 8, 8), 8), :] = value
        return carry

    lax.fori_loop(0, 32, one, 0)


def finish(parts_ref, coarse_ref, scores_ref, moved_ref):
    total = parts_ref[pl.ds(0, 512, stride=8), :]
    for s in range(1, 8):
        total = total + parts_ref[pl.ds(s, 512, stride=8), :]
    picked = lax.broadcasted_iota(jnp.int32, (8, 128), 1) // GROUP
    picked = (picked == lax.broadcasted_iota(jnp.int32, (8, 128), 0)).astype(jnp.float32)
    sums = lax.dot_general(
        picked,
        total,
        (((1,), (1,)), ((), ())),
        precision=lax.Precision.HIGHEST,
        preferred_element_type=jnp.float32,
    ) * (1.0 / CELLS)
    tiles = [sums[:, 128 * i : 128 * (i + 1)] for i in range(4)]
    lane = lax.broadcasted_iota(jnp.int32, (8, 128), 1)
    own = jnp.where(lane >= 3 * GROUP, tiles[3], 0.0)
    own = own + pltpu.roll(own, 64, 1)
    own = own + pltpu.roll(own, 32, 1) + EPS
    scored = [
        CELLS**0.5 * tiles[i] / jnp.sqrt(own * (tiles[2 + i] + EPS)) for i in range(2)
    ]
    scores = [
        scored[k // 4] if k % 4 == 0 else pltpu.roll(scored[k // 4], 128 - GROUP * (k % 4), 1)
        for k in range(7)
    ]

    def tile(value, bx):
        value = value if bx == 0 else pltpu.roll(value, 128 - 8 * bx, 1)
        return value[:BLOCKS, :8]

    for k in range(7):
        for bx in range(4):
            scores_ref[k, bx] = tile(scores[k], bx)
    for a in range(3):
        low, high = scores[1 + 2 * a], scores[2 + 2 * a]
        curvature = jnp.maximum(2.0 * scores[0] - low - high, 1.0)
        step = (high - low) / (2.0 * curvature)
        for bx in range(4):
            moved_ref[a, bx] = coarse_ref[a, bx].astype(jnp.float32) + tile(step, bx)


def local_kernel(
    shift_ref, migration_ref, samples_ref, column_ref, depth_ref, coarse_ref,
    scores_ref, moved_ref, gain_ref, image_ref, volume_ref, parts_ref,
):
    expand_gain(column_ref, gain_ref)
    clear(volume_ref)
    make_images(migration_ref, samples_ref, gain_ref, depth_ref, image_ref, volume_ref)
    correlate(image_ref, volume_ref, shift_ref, parts_ref)
    finish(parts_ref, coarse_ref, scores_ref, moved_ref)


def local_stage(migration, samples, column_gain, depth_rows, coarse):
    vmem = pl.BlockSpec(memory_space=pltpu.VMEM)
    smem = pl.BlockSpec(memory_space=pltpu.SMEM)
    return pl.pallas_call(
        local_kernel,
        out_shape=(
            jax.ShapeDtypeStruct((7, 4, 4, 8), jnp.float32),
            jax.ShapeDtypeStruct((3, 4, 4, 8), jnp.float32),
        ),
        in_specs=[smem, vmem, vmem, vmem, vmem, vmem],
        out_specs=(vmem, vmem),
        scratch_shapes=[
            pltpu.VMEM((LX * LY, 128), jnp.float32),
            pltpu.VMEM((LX * LY, 128), jnp.float32),
            pltpu.VMEM((LX + 2 * MARGIN, LY + 2 * YPAD, 128), jnp.float32),
            pltpu.VMEM((16 * 32 * 8, 128), jnp.float32),
        ],
        compiler_params=pltpu.CompilerParams(vmem_limit_bytes=40 * 2**20),
    )(coarse, migration, samples, column_gain.reshape(16, 128), depth_rows, coarse)


def with_sides(array):
    n = lax.axis_size("slab")
    up = [(i, i + 1) for i in range(n - 1)]
    down = [(i + 1, i) for i in range(n - 1)]
    before = lax.ppermute(array[:, -MARGIN:], "slab", up)
    after = lax.ppermute(array[:, :MARGIN], "slab", down)
    return jnp.concatenate([before, array, after], axis=1)


def per_device(element_data, migration, column_gain, depth_gain, coarse_shift, reference_frame):
    elements, _, depth = element_data.shape
    data = element_data.reshape(elements, depth)
    chosen = lax.axis_index("frame") == reference_frame[0]
    own = lax.all_to_all(data, "slab", split_axis=1, concat_axis=0, tiled=True)
    shared = lax.psum(jnp.where(chosen, own, 0).astype(jnp.bfloat16), "frame")
    shared = with_sides(shared)

    def spread(columns):
        groups = [
            jnp.pad(columns[:, KZ * b : KZ * (b + 1)], ((0, 0), (1, GROUP - KZ - 1)))
            for b in range(BLOCKS)
        ]
        return jnp.concatenate(groups, axis=1)

    def fill(columns):
        return jnp.pad(columns, ((0, 0), (0, 128 - columns.shape[1])))

    samples = jnp.concatenate([spread(own), fill(shared)], axis=1)
    gains = depth_gain[None, :]
    depth_rows = jnp.concatenate([spread(gains), fill(with_sides(gains))], axis=0)
    coarse = coarse_shift[:, 0].transpose(0, 1, 3, 2)
    scores, moved = local_stage(migration, samples, column_gain, depth_rows, coarse)
    return scores.transpose(0, 1, 3, 2)[:, None], moved.transpose(0, 1, 3, 2)[:, None]


def solution(mesh):
    placed = (
        P("slab", "frame", None),
        P(),
        P(),
        P("slab"),
        P(None, "frame", None, None, "slab"),
        P(),
    )
    return jax.shard_map(
        per_device,
        mesh=mesh,
        in_specs=placed,
        out_specs=(P(None, "frame", None, None, "slab"), P(None, "frame", None, None, "slab")),
        check_vma=False,
    )
```

time: 596 us -> 117 us (0.20)
  the two profiles are of different devices: /device:TPU:1 before, /device:TPU:2 now
where the time goes in v1:
time: 117 us
  waiting for transfers between devices  43.2 us (37%)
  starting transfers between devices  35.4 us (30%)
  between operations  14.8 us (13%)
  Pallas kernels  12.7 us (11%)
  local copies, waits for them, and re-layouts  8.9 us (8%)
  other arithmetic  1.85 us (2%)
    psum x1, waiting for transfers between devices, per_device(): shared = lax.psum(jnp.where(chosen, own, 0).astype(jnp.bfloat16), 'frame')  38.2 us
    all_to_all x1, starting transfers between devices, per_device(): own = lax.all_to_all(data, 'slab', split_axis=1, concat_axis=0, tiled=True)  14.7 us
    ppermute x2, starting transfers between devices, with_sides(): after = lax.ppermute(array[:, :MARGIN], 'slab', down)  13.9 us
    pallas_call x1, Pallas kernels, local_stage(): pl.pallas_call(local_kernel, out_shape=(jax.ShapeDtypeStruct((7, 4, 4, 8)...  12.7 us
    ppermute x2, starting transfers between devices, with_sides(): before = lax.ppermute(array[:, -MARGIN:], 'slab', up)  6.82 us
    ppermute x2, waiting for transfers between devices, with_sides(): before = lax.ppermute(array[:, -MARGIN:], 'slab', up)  3.73 us
    unnamed x10, local copies, waits for them, and re-layouts  3.26 us
  transfers between devices with their start and end apart: 6, of which 3 were waited for; matrix products, arithmetic and copies ran while one was open for 4% of the time, Pallas kernels for 0%

profile of v1, /device:TPU:2, one launch (start us, length us, event | category | flops | bytes accessed | tf_op | source)
XLA Modules:
  0.0 116.9 jit_solution(9540520883393759391)
XLA Ops:
  7.2 1.2 %all_to_all.14 = bf16[16,64,64]{2,1,0:T(8,128)(2,1)S(1)} reshape(bf16[16,1,4096]{2,0,1:T(8,128)(2,1)} %param.6) | data formatting | bytes 262144 | tf_op jit(solution)/shard_map/all_to_all | solution.py:216
  8.3 0.2 copy.12
  8.5 0.8 reshape.13
  9.4 14.7 %all-to-all-start = ((bf16[64,2,512]{2,1,0:T(2,128)(2,1)}), bf16[64,2,512]{2,1,0:T(2,128)(2,1)S(1)}, u32[]{:S(2)}, u32[]{:S(2)}) async-start(bf16[64,2,512]{2,1,0:T(2,128)(2,1)} %reshape.13), calls=%async_computation | async-start | bytes 262144 | tf_op jit(solution)/shard_map/all_to_all | solution.py:216
  24.1 0.8 fusion.11
  24.9 3.4 %collective-permute-start.2 = (f32[1,9]{1,0:T(1,128)S(1)}, f32[1,9]{1,0:T(1,128)S(1)}, u32[]{:S(2)}, u32[]{:S(2)}) collective-permute-start(f32[1,9]{1,0:T(1,128)S(1)} %get-tuple-element.14), channel_id=1, source_target_pairs={{0,1},{1,2},{2,3},{3,4},{4,5},{5,6},{6,7},{7,8},{8,9},{9,10},{10,1... | collective-permute-start | bytes 116 | tf_op jit(solution)/shard_map/ppermute | solution.py:207
  28.3 7.0 %collective-permute-start.3 = (f32[1,9]{1,0:T(1,128)S(1)}, f32[1,9]{1,0:T(1,128)S(1)}, u32[]{:S(2)}, u32[]{:S(2)}) collective-permute-start(f32[1,9]{1,0:T(1,128)S(1)} %get-tuple-element.15), channel_id=1, source_target_pairs={{1,0},{2,1},{3,2},{4,3},{5,4},{6,5},{7,6},{8,7},{9,8},{10,9},{11,1... | collective-permute-start | bytes 116 | tf_op jit(solution)/shard_map/ppermute | solution.py:208
  35.9 0.9 fusion.12
  36.8 0.2 reshape.14
  37.0 0.7 broadcast_select_fusion
  37.8 0.7 select_maximum_fusion
  38.6 38.2 %all-reduce.12.cloned.1.call-done = bf16[1024,64]{1,0:T(8,128)(2,1)} async-done(((bf16[1024,64]{1,0:T(8,128)(2,1)}), bf16[1024,64]{1,0:T(8,128)(2,1)}) %all-reduce.12.cloned.1.call-update) | async-done | bytes 131088 | tf_op jit(solution)/shard_map/psum | solution.py:217
  76.9 1.2 %fusion.9 = (bf16[1024,9]{1,0:T(8,128)(2,1)S(1)}, bf16[1024,9]{1,0:T(8,128)(2,1)S(1)}) fusion(bf16[1024,64]{1,0:T(8,128)(2,1)} %all-reduce.12.cloned.1.call-done), kind=kLoop, calls=%fused_computation.18 | loop fusion | bytes 73728 | tf_op jit(solution)/shard_map/slice | solution.py:207
  78.1 3.5 %collective-permute-start = (bf16[1024,9]{1,0:T(8,128)(2,1)S(1)}, bf16[1024,9]{1,0:T(8,128)(2,1)S(1)}, u32[]{:S(2)}, u32[]{:S(2)}) collective-permute-start(bf16[1024,9]{1,0:T(8,128)(2,1)S(1)} %get-tuple-element.8), channel_id=1, source_target_pairs={{0,1},{1,2},{2,3},{3,4},{4,5},{5,6},{6,7},{7,8},{8,9},{9,10},{10,1... | collective-permute-start | bytes 55304 | tf_op jit(solution)/shard_map/ppermute | solution.py:207
  81.6 6.9 %collective-permute-start.1 = (bf16[1024,9]{1,0:T(8,128)(2,1)S(1)}, bf16[1024,9]{1,0:T(8,128)(2,1)S(1)}, u32[]{:S(2)}, u32[]{:S(2)}) collective-permute-start(bf16[1024,9]{1,0:T(8,128)(2,1)S(1)} %get-tuple-element.9), channel_id=1, source_target_pairs={{1,0},{2,1},{3,2},{4,3},{5,4},{6,5},{7,6},{8,7},{9,8},{10,9},{11,1... | collective-permute-start | bytes 55304 | tf_op jit(solution)/shard_map/ppermute | solution.py:208
  88.5 0.3 fusion.10
  89.0 0.1 pad.35
  89.2 0.1 pad.34
  89.3 3.7 %collective-permute-done = bf16[1024,9]{1,0:T(8,128)(2,1)S(1)} collective-permute-done((bf16[1024,9]{1,0:T(8,128)(2,1)S(1)}, bf16[1024,9]{1,0:T(8,128)(2,1)S(1)}, u32[]{:S(2)}, u32[]{:S(2)}) %collective-permute-start) | collective-permute-done | bytes 18464 | tf_op jit(solution)/shard_map/ppermute | solution.py:207
  93.0 1.2 %collective-permute-done.1 = bf16[1024,9]{1,0:T(8,128)(2,1)S(1)} collective-permute-done((bf16[1024,9]{1,0:T(8,128)(2,1)S(1)}, bf16[1024,9]{1,0:T(8,128)(2,1)S(1)}, u32[]{:S(2)}, u32[]{:S(2)}) %collective-permute-start.1) | collective-permute-done | bytes 18464 | tf_op jit(solution)/shard_map/ppermute | solution.py:208
  94.2 0.3 fusion.4
  94.5 0.6 concatenate.16.samples_ref
  95.1 2.2 %copy-done = bf16[2048,1024]{1,0:T(8,128)(2,1)S(1)} copy-done((bf16[2048,1024]{1,0:T(8,128)(2,1)S(1)}, bf16[2048,1024]{1,0:T(8,128)(2,1)}, u32[]{:S(2)}) %copy-start) | copy-done | bytes 4194328
  97.3 12.7 %shard_map.77 = (f32[7,4,4,8]{3,2,1,0:T(4,128)}, f32[3,4,4,8]{3,2,1,0:T(4,128)}) custom-call(s32[3,4,4,8]{3,2,1,0:T(4,128)S(1)} %bitcast.27, bf16[2048,1024]{1,0:T(8,128)(2,1)S(1)} %copy-done, bf16[1024,256]{1,0:T(8,128)(2,1)S(1)} %concatenate.16.samples_ref, f32[16,128]{1,0:T(8,128)S(1)} %bitcast.29, f32[2,128]{1,0:T(2,128)S(1)} %fusion.8.depth_ref, ...), custom_call_target="tpu_custom_call" | custom-call | tf_op jit(solution)/shard_map/pallas_call | solution.py:185
  (15 shorter events, 0.4 us)
Async XLA Ops:
  9.4 27.4 %all-to-all-start = ((bf16[64,2,512]{2,1,0:T(2,128)(2,1)}), bf16[64,2,512]{2,1,0:T(2,128)(2,1)S(1)}, u32[]{:S(2)}, u32[]{:S(2)}) async-start(bf16[64,2,512]{2,1,0:T(2,128)(2,1)} %reshape.13), calls=%async_computation | async-start | bytes 262144 | tf_op jit(solution)/shard_map/all_to_all | solution.py:216
  24.0 52.8 %all-reduce.12.cloned.1.call-start = ((), (), s32[]{:S(2)}) async-start(), calls=%async_computation.1 | async-start | bytes 524288 | tf_op jit(solution)/shard_map/psum | solution.py:217
  24.9 12.9 %collective-permute-start.2 = (f32[1,9]{1,0:T(1,128)S(1)}, f32[1,9]{1,0:T(1,128)S(1)}, u32[]{:S(2)}, u32[]{:S(2)}) collective-permute-start(f32[1,9]{1,0:T(1,128)S(1)} %get-tuple-element.14), channel_id=1, source_target_pairs={{0,1},{1,2},{2,3},{3,4},{4,5},{5,6},{6,7},{7,8},{8,9},{9,10},{10,1... | collective-permute-start | bytes 116 | tf_op jit(solution)/shard_map/ppermute | solution.py:207
  28.3 9.5 %collective-permute-start.3 = (f32[1,9]{1,0:T(1,128)S(1)}, f32[1,9]{1,0:T(1,128)S(1)}, u32[]{:S(2)}, u32[]{:S(2)}) collective-permute-start(f32[1,9]{1,0:T(1,128)S(1)} %get-tuple-element.15), channel_id=1, source_target_pairs={{1,0},{2,1},{3,2},{4,3},{5,4},{6,5},{7,6},{8,7},{9,8},{10,9},{11,1... | collective-permute-start | bytes 116 | tf_op jit(solution)/shard_map/ppermute | solution.py:208
  37.8 57.3 %copy-start.1 = (s32[3,1,4,8,4]{3,4,2,1,0:T(4,128)S(1)}, s32[3,1,4,8,4]{3,4,2,1,0:T(4,128)}, u32[]{:S(2)}) copy-start(s32[3,1,4,8,4]{3,4,2,1,0:T(4,128)} %param.10) | copy-start | bytes 4612
  37.8 57.4 %copy-start.2 = (f32[2048]{0:T(1024)S(1)}, f32[2048]{0:T(1024)}, u32[]{:S(2)}) copy-start(f32[2048]{0:T(1024)} %param.8) | copy-start | bytes 24580
  76.9 17.4 %copy-start.3 = (bf16[1024,64]{1,0:T(8,128)(2,1)S(1)}, bf16[1024,64]{1,0:T(8,128)(2,1)}, u32[]{:S(2)}) copy-start(bf16[1024,64]{1,0:T(8,128)(2,1)} %all-reduce.12.cloned.1.call-done) | copy-start | bytes 393220
  78.1 15.0 %collective-permute-start = (bf16[1024,9]{1,0:T(8,128)(2,1)S(1)}, bf16[1024,9]{1,0:T(8,128)(2,1)S(1)}, u32[]{:S(2)}, u32[]{:S(2)}) collective-permute-start(bf16[1024,9]{1,0:T(8,128)(2,1)S(1)} %get-tuple-element.8), channel_id=1, source_target_pairs={{0,1},{1,2},{2,3},{3,4},{4,5},{5,6},{6,7},{7,8},{8,9},{9,10},{10,1... | collective-permute-start | bytes 55304 | tf_op jit(solution)/shard_map/ppermute | solution.py:207
  81.6 12.7 %collective-permute-start.1 = (bf16[1024,9]{1,0:T(8,128)(2,1)S(1)}, bf16[1024,9]{1,0:T(8,128)(2,1)S(1)}, u32[]{:S(2)}, u32[]{:S(2)}) collective-permute-start(bf16[1024,9]{1,0:T(8,128)(2,1)S(1)} %get-tuple-element.9), channel_id=1, source_target_pairs={{1,0},{2,1},{3,2},{4,3},{5,4},{6,5},{7,6},{8,7},{9,8},{10,9},{11,1... | collective-permute-start | bytes 55304 | tf_op jit(solution)/shard_map/ppermute | solution.py:208
  95.1 2.2 %copy-start = (bf16[2048,1024]{1,0:T(8,128)(2,1)S(1)}, bf16[2048,1024]{1,0:T(8,128)(2,1)}, u32[]{:S(2)}) copy-start(bf16[2048,1024]{1,0:T(8,128)(2,1)} %migration_ref.1) | copy-start | bytes 12582916
Sparse Core Ops, SparseCore 0:
  37.9 38.9 all-reduce.11

commit v2 on v1

--- a/solution.py
+++ b/solution.py
@@ -16,6 +16,8 @@
 EPS = 1e-5
 CELLS = KX * KY * KZ
 ROWS = 256
+ELEMENTS = 16
+MESH = pl.DeviceIdType.MESH
 
 
 def expand_gain(gain_ref, wide_ref):
@@ -30,24 +32,6 @@
         return carry
 
     lax.fori_loop(0, volume_ref.shape[0], one, 0)
-
-
-def make_images(migration_ref, samples_ref, gain_ref, depth_ref, image_ref, volume_ref):
-    planes = ROWS // LY
-
-    def one(i, carry):
-        rows = pl.ds(pl.multiple_of(i * ROWS, ROWS), ROWS)
-        raw = jnp.dot(migration_ref[rows, :], samples_ref[...], preferred_element_type=jnp.float32)
-        gain = gain_ref[rows, :]
-        own = (raw[:, :128] * gain * depth_ref[0:1, :]).astype(jnp.bfloat16)
-        image_ref[rows, :] = own.astype(jnp.float32)
-        ref = (raw[:, 128:] * gain * depth_ref[1:2, :]).astype(jnp.bfloat16)
-        ref = ref.astype(jnp.float32)
-        for j in range(planes):
-            volume_ref[MARGIN + i * planes + j, YPAD : YPAD + LY, :] = ref[j * LY : (j + 1) * LY]
-        return carry
-
-    lax.fori_loop(0, LX * LY // ROWS, one, 0)
 
 
 def correlate(image_ref, volume_ref, shift_ref, parts_ref):
@@ -168,70 +152,303 @@
             moved_ref[a, bx] = coarse_ref[a, bx].astype(jnp.float32) + tile(step, bx)
 
 
-def local_kernel(
-    shift_ref, migration_ref, samples_ref, column_ref, depth_ref, coarse_ref,
-    scores_ref, moved_ref, gain_ref, image_ref, volume_ref, parts_ref,
+def scaled(migration_ref, samples, gain_ref, depth_row, i):
+    rows = pl.ds(pl.multiple_of(i * ROWS, ROWS), ROWS)
+    raw = jnp.dot(migration_ref[rows, :], samples, preferred_element_type=jnp.float32)
+    return (raw * gain_ref[rows, :] * depth_row).astype(jnp.bfloat16).astype(jnp.float32)
+
+
+def make_image(migration_ref, samples_ref, gain_ref, depth_ref, image_ref):
+    def one(i, carry):
+        rows = pl.ds(pl.multiple_of(i * ROWS, ROWS), ROWS)
+        image_ref[rows, :] = scaled(migration_ref, samples_ref[...], gain_ref, depth_ref[0:1, :], i)
+        return carry
+
+    lax.fori_loop(0, LX * LY // ROWS, one, 0)
+
+
+def make_volume(migration_ref, samples_ref, gain_ref, depth_ref, volume_ref):
+    planes = ROWS // LY
+
+    def one(i, carry):
+        samples = samples_ref[...].reshape(-1, 128)
+        ref = scaled(migration_ref, samples, gain_ref, depth_ref[1:2, :], i)
+        for j in range(planes):
+            volume_ref[MARGIN + i * planes + j, YPAD : YPAD + LY, :] = ref[j * LY : (j + 1) * LY]
+        return carry
+
+    lax.fori_loop(0, LX * LY // ROWS, one, 0)
+
+
+def place_of(column):
+    return GROUP * (column // KZ) + 1 + column % KZ
+
+
+def spread_depth(gains_ref, depth_ref):
+    lane = lax.broadcasted_iota(jnp.int32, (8, 128), 1)
+    left, here, right = [jnp.broadcast_to(gains_ref[i], (8, 128)) for i in range(3)]
+    row = jnp.zeros((8, 128), jnp.float32)
+    for b in range(BLOCKS):
+        turned = pltpu.roll(here, (GROUP * b + 1 - KZ * b) % 128, 1)
+        start = GROUP * b + 1
+        row = jnp.where((lane >= start) & (lane < start + KZ), turned, row)
+    sides = jnp.where(lane < MARGIN, pltpu.roll(left, 128 - 64 + MARGIN, 1), 0.0)
+    sides = jnp.where((lane >= MARGIN) & (lane < MARGIN + 64), pltpu.roll(here, MARGIN, 1), sides)
+    sides = jnp.where(
+        (lane >= MARGIN + 64) & (lane < 2 * MARGIN + 64), pltpu.roll(right, MARGIN + 64, 1), sides
+    )
+    depth_ref[0:1, :] = row[0:1]
+    depth_ref[1:2, :] = sides[0:1]
+
+
+def pack_own(data_ref, send_ref):
+    low = lax.broadcasted_iota(jnp.int32, (8, 128), 1) < 64
+    for t in range(send_ref.shape[0] // 2):
+        tile = data_ref[:, 128 * (t + 1) : 128 * (t + 2)].astype(jnp.float32)
+        first, second = tile[:8], tile[8:]
+        even = jnp.where(low, first, pltpu.roll(second, 64, 1))
+        odd = jnp.where(low, pltpu.roll(first, 64, 1), second)
+        send_ref[2 * t] = even.astype(jnp.bfloat16)
+        send_ref[2 * t + 1] = odd.astype(jnp.bfloat16)
+
+
+def unpack_own(recv_ref, samples_ref):
+    row = lax.broadcasted_iota(jnp.int32, (128, 128), 0)
+    lane = lax.broadcasted_iota(jnp.int32, (128, 128), 1)
+    packed = recv_ref[...].astype(jnp.float32).reshape(-1, 128).astype(jnp.bfloat16)
+    halves = []
+    for start in (0, 64):
+        column = row - start
+        picked = (lane == place_of(column)) & (column >= 0) & (column < 64)
+        picked = picked.astype(jnp.float32).astype(jnp.bfloat16)
+        half = jnp.dot(packed, picked, preferred_element_type=jnp.float32)
+        halves.append(half.reshape(-1, 8, 128))
+    samples = jnp.concatenate(halves, axis=1).reshape(-1, 128)
+    samples_ref[...] = samples.astype(jnp.bfloat16)
+
+
+def pack_reference(quarters_ref, chosen, send_ref):
+    lane = lax.broadcasted_iota(jnp.int32, (ELEMENTS, 128), 1)
+    tiles = quarters_ref.shape[2] // 128
+    parts = [quarters_ref[chosen, :, 128 * t : 128 * (t + 1)].astype(jnp.float32) for t in range(tiles)]
+    for m in range(tiles - 2):
+        for half in (0, 1):
+            turn = MARGIN + 64 * half
+            here, after = parts[m + half], parts[m + half + 1]
+            window = jnp.where(lane < turn, pltpu.roll(here, turn, 1), pltpu.roll(after, turn, 1))
+            send_ref[2 * m + half] = window.astype(jnp.bfloat16)
+
+
+def fused_kernel(
+    slabs, frames,
+    shift_ref, chosen_ref, data_hbm, migration_hbm, column_ref, gains_in_ref, coarse_ref,
+    scores_ref, moved_ref,
+    data_ref, migration_ref, own_send, own_recv, quarters_ref, ref_send, ref_recv,
+    gains_ref, gain_ref, depth_ref, samples_ref, image_ref, volume_ref, parts_ref,
+    local_sems, own_sems, quarter_send_sems, quarter_recv_sems, ref_sems, gain_send_sems, gain_recv_sems,
 ):
+    frame = lax.axis_index("frame")
+    slab = lax.axis_index("slab")
+    share = slabs // frames
+    source = slab // share
+    same = jnp.where(source == frame, 1, 0)
+
+    gains_ref[...] = jnp.zeros(gains_ref.shape, gains_ref.dtype)
+    gains_ref[1, :, :64] = gains_in_ref[...]
+    barrier = pltpu.get_barrier_semaphore()
+
+    def greet(target_frame, target_slab):
+        pl.semaphore_signal(
+            barrier, inc=1, device_id={"frame": target_frame, "slab": target_slab}, device_id_type=MESH
+        )
+
+    def greet_own(i, carry):
+        greet(frame, (slab + 1 + i) % slabs)
+        return carry
+
+    def greet_source(i, carry):
+        other = (slab + i) % slabs
+
+        @pl.when((other != slab) | (source != frame))
+        def _():
+            greet(source, other)
+
+        return carry
+
+    for i in range(1, frames):
+        greet((frame + i) % frames, slab)
+    lax.fori_loop(0, slabs - 1, greet_own, 0)
+    lax.fori_loop(0, slabs, greet_source, 0)
+
+    data_ref[:, :128] = jnp.zeros((ELEMENTS, 128), data_ref.dtype)
+    data_ref[:, -128:] = jnp.zeros((ELEMENTS, 128), data_ref.dtype)
+    width = data_hbm.shape[1]
+    load_data = pltpu.make_async_copy(data_hbm, data_ref.at[:, pl.ds(128, width)], local_sems.at[0])
+    load_data.start()
+    load_migration = pltpu.make_async_copy(migration_hbm, migration_ref, local_sems.at[1])
+    load_migration.start()
+
+    load_data.wait()
+    pl.semaphore_wait(barrier, (frames - 1) + (slabs - 1) + slabs - same)
+
+    quarter = width // frames
+
+    def quarter_of(i):
+        return data_ref.at[:, pl.ds(pl.multiple_of(i * quarter, 128), quarter + 256)]
+
+    quarter_copies = []
+    for i in range(1, frames):
+        other = (frame + i) % frames
+        copy = pltpu.make_async_remote_copy(
+            src_ref=quarter_of(other),
+            dst_ref=quarters_ref.at[frame],
+            send_sem=quarter_send_sems.at[i - 1],
+            recv_sem=quarter_recv_sems.at[i - 1],
+            device_id={"frame": other},
+            device_id_type=MESH,
+        )
+        copy.start()
+        quarter_copies.append(copy)
+    keep_quarter = pltpu.make_async_copy(quarter_of(frame), quarters_ref.at[frame], local_sems.at[2])
+    keep_quarter.start()
+
+    pack_own(data_ref, own_send)
+
+    def send_own(i, carry):
+        other = (slab + 1 + i) % slabs
+        pltpu.make_async_remote_copy(
+            src_ref=own_send.at[other],
+            dst_ref=own_recv.at[slab],
+            send_sem=own_sems.at[0],
+            recv_sem=own_sems.at[1],
+            device_id={"slab": other},
+            device_id_type=MESH,
+        ).start()
+        return carry
+
+    lax.fori_loop(0, slabs - 1, send_own, 0)
+    pltpu.make_async_copy(own_send.at[slab], own_recv.at[slab], own_sems.at[1]).start()
+
+    def gain_copy(way, other):
+        return pltpu.make_async_remote_copy(
+            src_ref=gains_ref.at[1],
+            dst_ref=gains_ref.at[1 - way],
+            send_sem=gain_send_sems.at[max(way, 0)],
+            recv_sem=gain_recv_sems.at[max(way, 0)],
+            device_id={"slab": other},
+            device_id_type=MESH,
+        )
+
+    to_next = gain_copy(1, (slab + 1) % slabs)
+    to_previous = gain_copy(-1, (slab + slabs - 1) % slabs)
+    has_next = slab < slabs - 1
+    has_previous = slab > 0
+    pl.when(has_next)(to_next.start)
+    pl.when(has_previous)(to_previous.start)
+
+    for copy in quarter_copies:
+        copy.wait_recv()
+    keep_quarter.wait()
+    pack_reference(quarters_ref, chosen_ref[0], ref_send)
+
+    def send_reference(i, carry):
+        place = (slab + i // frames) % share
+        to_frame = (frame + i) % frames
+        to_slab = frame * share + place
+        here = (to_frame == frame) & (to_slab == slab)
+
+        @pl.when(jnp.logical_not(here))
+        def _():
+            pltpu.make_async_remote_copy(
+                src_ref=ref_send.at[place],
+                dst_ref=ref_recv.at[slab],
+                send_sem=ref_sems.at[0],
+                recv_sem=ref_sems.at[1],
+                device_id={"frame": to_frame, "slab": to_slab},
+                device_id_type=MESH,
+            ).start()
+
+        return carry
+
+    lax.fori_loop(0, slabs, send_reference, 0)
+
+    @pl.when(source == frame)
+    def _():
+        pltpu.make_async_copy(ref_send.at[slab % share], ref_recv.at[slab], ref_sems.at[1]).start()
+
     expand_gain(column_ref, gain_ref)
     clear(volume_ref)
-    make_images(migration_ref, samples_ref, gain_ref, depth_ref, image_ref, volume_ref)
+    pl.when(has_previous)(to_next.wait_recv)
+    pl.when(has_next)(to_previous.wait_recv)
+    spread_depth(gains_ref, depth_ref)
+    load_migration.wait()
+    pltpu.make_async_copy(own_recv, own_recv, own_sems.at[1]).wait()
+    unpack_own(own_recv, samples_ref)
+    make_image(migration_ref, samples_ref, gain_ref, depth_ref, image_ref)
+    pltpu.make_async_copy(ref_recv, ref_recv, ref_sems.at[1]).wait()
+    make_volume(migration_ref, ref_recv, gain_ref, depth_ref, volume_ref)
     correlate(image_ref, volume_ref, shift_ref, parts_ref)
     finish(parts_ref, coarse_ref, scores_ref, moved_ref)
 
-
-def local_stage(migration, samples, column_gain, depth_rows, coarse):
+    for copy in quarter_copies:
+        copy.wait_send()
+    pl.when(has_next)(to_next.wait_send)
+    pl.when(has_previous)(to_previous.wait_send)
+    most = pl.ds(0, slabs - 1)
+    pltpu.make_async_copy(own_recv.at[most], own_recv.at[most], own_sems.at[0]).wait()
+
+    @pl.when(source == frame)
+    def _():
+        pltpu.make_async_copy(ref_recv.at[most], ref_recv.at[most], ref_sems.at[0]).wait()
+
+    @pl.when(source != frame)
+    def _():
+        pltpu.make_async_copy(ref_recv, ref_recv, ref_sems.at[0]).wait()
+
+
+def per_device(slabs, frames, element_data, migration, column_gain, depth_gain, coarse_shift, reference_frame):
+    elements, _, depth = element_data.shape
+    data = element_data.reshape(elements, depth)
+    coarse = coarse_shift[:, 0].transpose(0, 1, 3, 2)
     vmem = pl.BlockSpec(memory_space=pltpu.VMEM)
     smem = pl.BlockSpec(memory_space=pltpu.SMEM)
-    return pl.pallas_call(
-        local_kernel,
+    hbm = pl.BlockSpec(memory_space=pl.ANY)
+    bf16, f32 = jnp.bfloat16, jnp.float32
+    scores, moved = pl.pallas_call(
+        functools.partial(fused_kernel, slabs, frames),
         out_shape=(
-            jax.ShapeDtypeStruct((7, 4, 4, 8), jnp.float32),
-            jax.ShapeDtypeStruct((3, 4, 4, 8), jnp.float32),
+            jax.ShapeDtypeStruct((7, 4, 4, 8), f32),
+            jax.ShapeDtypeStruct((3, 4, 4, 8), f32),
         ),
-        in_specs=[smem, vmem, vmem, vmem, vmem, vmem],
+        in_specs=[smem, smem, hbm, hbm, vmem, vmem, vmem],
         out_specs=(vmem, vmem),
         scratch_shapes=[
-            pltpu.VMEM((LX * LY, 128), jnp.float32),
-            pltpu.VMEM((LX * LY, 128), jnp.float32),
-            pltpu.VMEM((LX + 2 * MARGIN, LY + 2 * YPAD, 128), jnp.float32),
-            pltpu.VMEM((16 * 32 * 8, 128), jnp.float32),
+            pltpu.VMEM((elements, depth + 256), bf16),
+            pltpu.VMEM(migration.shape, bf16),
+            pltpu.VMEM((slabs, 8, 128), bf16),
+            pltpu.VMEM((slabs, 8, 128), bf16),
+            pltpu.VMEM((frames, elements, depth // frames + 256), bf16),
+            pltpu.VMEM((slabs // frames, elements, 128), bf16),
+            pltpu.VMEM((slabs, elements, 128), bf16),
+            pltpu.VMEM((3, 1, 128), f32),
+            pltpu.VMEM((LX * LY, 128), f32),
+            pltpu.VMEM((8, 128), f32),
+            pltpu.VMEM((slabs * elements, 128), bf16),
+            pltpu.VMEM((LX * LY, 128), f32),
+            pltpu.VMEM((LX + 2 * MARGIN, LY + 2 * YPAD, 128), f32),
+            pltpu.VMEM((16 * 32 * 8, 128), f32),
+            pltpu.SemaphoreType.DMA((3,)),
+            pltpu.SemaphoreType.DMA((2,)),
+            pltpu.SemaphoreType.DMA((frames - 1,)),
+            pltpu.SemaphoreType.DMA((frames - 1,)),
+            pltpu.SemaphoreType.DMA((2,)),
+            pltpu.SemaphoreType.DMA((2,)),
+            pltpu.SemaphoreType.DMA((2,)),
         ],
-        compiler_params=pltpu.CompilerParams(vmem_limit_bytes=40 * 2**20),
-    )(coarse, migration, samples, column_gain.reshape(16, 128), depth_rows, coarse)
-
-
-def with_sides(array):
-    n = lax.axis_size("slab")
-    up = [(i, i + 1) for i in range(n - 1)]
-    down = [(i + 1, i) for i in range(n - 1)]
-    before = lax.ppermute(array[:, -MARGIN:], "slab", up)
-    after = lax.ppermute(array[:, :MARGIN], "slab", down)
-    return jnp.concatenate([before, array, after], axis=1)
-
-
-def per_device(element_data, migration, column_gain, depth_gain, coarse_shift, reference_frame):
-    elements, _, depth = element_data.shape
-    data = element_data.reshape(elements, depth)
-    chosen = lax.axis_index("frame") == reference_frame[0]
-    own = lax.all_to_all(data, "slab", split_axis=1, concat_axis=0, tiled=True)
-    shared = lax.psum(jnp.where(chosen, own, 0).astype(jnp.bfloat16), "frame")
-    shared = with_sides(shared)
-
-    def spread(columns):
-        groups = [
-            jnp.pad(columns[:, KZ * b : KZ * (b + 1)], ((0, 0), (1, GROUP - KZ - 1)))
-            for b in range(BLOCKS)
-        ]
-        return jnp.concatenate(groups, axis=1)
-
-    def fill(columns):
-        return jnp.pad(columns, ((0, 0), (0, 128 - columns.shape[1])))
-
-    samples = jnp.concatenate([spread(own), fill(shared)], axis=1)
-    gains = depth_gain[None, :]
-    depth_rows = jnp.concatenate([spread(gains), fill(with_sides(gains))], axis=0)
-    coarse = coarse_shift[:, 0].transpose(0, 1, 3, 2)
-    scores, moved = local_stage(migration, samples, column_gain, depth_rows, coarse)
+        compiler_params=pltpu.CompilerParams(
+            collective_id=0, has_side_effects=True, vmem_limit_bytes=48 * 2**20
+        ),
+    )(coarse, reference_frame, data, migration, column_gain.reshape(16, 128), depth_gain.reshape(1, -1), coarse)
     return scores.transpose(0, 1, 3, 2)[:, None], moved.transpose(0, 1, 3, 2)[:, None]
 
 
@@ -245,7 +462,7 @@
         P(),
     )
     return jax.shard_map(
-        per_device,
+        functools.partial(per_device, mesh.shape["slab"], mesh.shape["frame"]),
         mesh=mesh,
         in_specs=placed,
         out_specs=(P(None, "frame", None, None, "slab"), P(None, "frame", None, None, "slab")),

time: 117 us -> 45.9 us (0.39)
  the two profiles are of different devices: /device:TPU:2 before, /device:TPU:1 now
where the time goes in v2:
time: 45.9 us; the launch traced here: 45.6 us
  Pallas kernels  37.9 us (83%)
  local copies, waits for them, and re-layouts  7.06 us (15%)
  between operations  0.65 us (1%)
    pallas_call x1, Pallas kernels, per_device(): pl.pallas_call(functools.partial(fused_kernel, slabs, frames), out_shape=...  37.9 us
    unnamed x14, local copies, waits for them, and re-layouts  7.06 us

profile of v2, /device:TPU:1, one launch (start us, length us, event | category | flops | bytes accessed | tf_op | source)
XLA Modules:
  0.0 45.6 jit_solution(6677249268914601627)
XLA Ops:
  0.6 0.0 copy-start
  0.6 2.2 %copy-done = bf16[2048,1024]{1,0:T(8,128)(2,1)S(1)} copy-done((bf16[2048,1024]{1,0:T(8,128)(2,1)S(1)}, bf16[2048,1024]{1,0:T(8,128)(2,1)}, u32[]{:S(2)}) %copy-start) | copy-done | bytes 4194328
  2.8 0.0 copy-start.1
  2.8 0.9 %copy-done.1 = bf16[16,1,4096]{2,0,1:T(8,128)(2,1)S(1)} copy-done((bf16[16,1,4096]{2,0,1:T(8,128)(2,1)S(1)}, bf16[16,1,4096]{2,0,1:T(8,128)(2,1)}, u32[]{:S(2)}) %copy-start.1) | copy-done | bytes 131096
  3.7 0.0 copy-start.2
  3.7 0.7 %copy-done.2 = s32[3,1,4,8,4]{3,4,2,1,0:T(4,128)S(1)} copy-done((s32[3,1,4,8,4]{3,4,2,1,0:T(4,128)S(1)}, s32[3,1,4,8,4]{3,4,2,1,0:T(4,128)}, u32[]{:S(2)}) %copy-start.2) | copy-done | bytes 1560
  4.5 0.0 copy-start.3
  4.5 0.7 %copy-done.3 = f32[2048]{0:T(1024)S(1)} copy-done((f32[2048]{0:T(1024)S(1)}, f32[2048]{0:T(1024)}, u32[]{:S(2)}) %copy-start.3) | copy-done | bytes 8216
  5.2 0.0 copy-start.4
  5.2 0.7 %copy-done.4 = s32[4]{0:T(128)S(1)} copy-done((s32[4]{0:T(128)S(1)}, s32[4]{0:T(128)}, u32[]{:S(2)}) %copy-start.4) | copy-done | bytes 40
  5.8 0.0 copy-start.5
  5.8 0.7 %copy-done.5 = f32[64]{0:T(128)S(1)} copy-done((f32[64]{0:T(128)S(1)}, f32[64]{0:T(128)}, u32[]{:S(2)}) %copy-start.5) | copy-done | bytes 280
  6.5 37.9 %shard_map.77 = (f32[7,4,4,8]{3,2,1,0:T(4,128)S(1)}, f32[3,4,4,8]{3,2,1,0:T(4,128)S(1)}) custom-call(s32[3,4,4,8]{3,2,1,0:T(4,128)S(1)} %bitcast.17, s32[4]{0:T(128)S(1)} %copy-done.4, bf16[16,4096]{1,0:T(8,128)(2,1)S(1)} %bitcast.16, bf16[2048,1024]{1,0:T(8,128)(2,1)S(1)} %copy-done, f32[16,128]{1,0:T(8,128)S(1)} %bitcast.21, f32[1,64]{1,0:T(1,128)S(1)} %bitcast.22, ...), custom_call_target="tpu_custom_call" | custom-call | tf_op jit(solution)/shard_map/pallas_call | solution.py:417
  44.4 0.6 %copy.12 = f32[7,1,4,8,4]{3,4,2,1,0:T(4,128)} copy(f32[7,1,4,8,4]{3,4,2,1,0:T(4,128)S(1)} %bitcast.19) | data formatting | bytes 7168
  45.0 0.6 %copy.13 = f32[3,1,4,8,4]{3,4,2,1,0:T(4,128)} copy(f32[3,1,4,8,4]{3,4,2,1,0:T(4,128)S(1)} %bitcast.20) | data formatting | bytes 3072
Async XLA Ops:
  0.6 2.2 %copy-start = (bf16[2048,1024]{1,0:T(8,128)(2,1)S(1)}, bf16[2048,1024]{1,0:T(8,128)(2,1)}, u32[]{:S(2)}) copy-start(bf16[2048,1024]{1,0:T(8,128)(2,1)} %migration_hbm.1) | copy-start | bytes 12582916
  2.8 0.9 %copy-start.1 = (bf16[16,1,4096]{2,0,1:T(8,128)(2,1)S(1)}, bf16[16,1,4096]{2,0,1:T(8,128)(2,1)}, u32[]{:S(2)}) copy-start(bf16[16,1,4096]{2,0,1:T(8,128)(2,1)} %param.6) | copy-start | bytes 393220
  3.7 0.7 %copy-start.2 = (s32[3,1,4,8,4]{3,4,2,1,0:T(4,128)S(1)}, s32[3,1,4,8,4]{3,4,2,1,0:T(4,128)}, u32[]{:S(2)}) copy-start(s32[3,1,4,8,4]{3,4,2,1,0:T(4,128)} %param.10) | copy-start | bytes 4612
  4.5 0.7 %copy-start.3 = (f32[2048]{0:T(1024)S(1)}, f32[2048]{0:T(1024)}, u32[]{:S(2)}) copy-start(f32[2048]{0:T(1024)} %param.8) | copy-start | bytes 24580
  5.2 0.7 %copy-start.4 = (s32[4]{0:T(128)S(1)}, s32[4]{0:T(128)}, u32[]{:S(2)}) copy-start(s32[4]{0:T(128)} %chosen_ref.1) | copy-start | bytes 52
  5.8 0.7 %copy-start.5 = (f32[64]{0:T(128)S(1)}, f32[64]{0:T(128)}, u32[]{:S(2)}) copy-start(f32[64]{0:T(128)} %param.9) | copy-start | bytes 772

commit v3 on v2

--- a/solution.py
+++ b/solution.py
@@ -241,8 +241,9 @@
 
 def fused_kernel(
     slabs, frames,
-    shift_ref, chosen_ref, data_hbm, migration_hbm, column_ref, gains_in_ref, coarse_ref,
+    shift_hbm, chosen_hbm, data_hbm, migration_hbm, column_hbm, gains_hbm,
     scores_ref, moved_ref,
+    shift_ref, chosen_ref, coarse_ref, column_ref, gains_in_ref,
     data_ref, migration_ref, own_send, own_recv, quarters_ref, ref_send, ref_recv,
     gains_ref, gain_ref, depth_ref, samples_ref, image_ref, volume_ref, parts_ref,
     local_sems, own_sems, quarter_send_sems, quarter_recv_sems, ref_sems, gain_send_sems, gain_recv_sems,
@@ -253,8 +254,24 @@
     source = slab // share
     same = jnp.where(source == frame, 1, 0)
 
+    width = data_hbm.shape[1]
+    loads = [
+        pltpu.make_async_copy(start, end, local_sems.at[i])
+        for i, (start, end) in enumerate(
+            (
+                (data_hbm, data_ref.at[:, pl.ds(128, width)]),
+                (gains_hbm, gains_in_ref),
+                (chosen_hbm, chosen_ref),
+                (migration_hbm, migration_ref),
+                (column_hbm, column_ref),
+                (shift_hbm, shift_ref),
+                (shift_hbm, coarse_ref),
+            )
+        )
+    ]
+    for copy in loads:
+        copy.start()
     gains_ref[...] = jnp.zeros(gains_ref.shape, gains_ref.dtype)
-    gains_ref[1, :, :64] = gains_in_ref[...]
     barrier = pltpu.get_barrier_semaphore()
 
     def greet(target_frame, target_slab):
@@ -282,13 +299,9 @@
 
     data_ref[:, :128] = jnp.zeros((ELEMENTS, 128), data_ref.dtype)
     data_ref[:, -128:] = jnp.zeros((ELEMENTS, 128), data_ref.dtype)
-    width = data_hbm.shape[1]
-    load_data = pltpu.make_async_copy(data_hbm, data_ref.at[:, pl.ds(128, width)], local_sems.at[0])
-    load_data.start()
-    load_migration = pltpu.make_async_copy(migration_hbm, migration_ref, local_sems.at[1])
-    load_migration.start()
-
-    load_data.wait()
+    for copy in loads[:3]:
+        copy.wait()
+    gains_ref[1, :, :64] = gains_in_ref[...]
     pl.semaphore_wait(barrier, (frames - 1) + (slabs - 1) + slabs - same)
 
     quarter = width // frames
@@ -309,7 +322,7 @@
         )
         copy.start()
         quarter_copies.append(copy)
-    keep_quarter = pltpu.make_async_copy(quarter_of(frame), quarters_ref.at[frame], local_sems.at[2])
+    keep_quarter = pltpu.make_async_copy(quarter_of(frame), quarters_ref.at[frame], local_sems.at[7])
     keep_quarter.start()
 
     pack_own(data_ref, own_send)
@@ -376,12 +389,13 @@
     def _():
         pltpu.make_async_copy(ref_send.at[slab % share], ref_recv.at[slab], ref_sems.at[1]).start()
 
+    for copy in loads[3:]:
+        copy.wait()
     expand_gain(column_ref, gain_ref)
     clear(volume_ref)
     pl.when(has_previous)(to_next.wait_recv)
     pl.when(has_next)(to_previous.wait_recv)
     spread_depth(gains_ref, depth_ref)
-    load_migration.wait()
     pltpu.make_async_copy(own_recv, own_recv, own_sems.at[1]).wait()
     unpack_own(own_recv, samples_ref)
     make_image(migration_ref, samples_ref, gain_ref, depth_ref, image_ref)
@@ -411,18 +425,23 @@
     data = element_data.reshape(elements, depth)
     coarse = coarse_shift[:, 0].transpose(0, 1, 3, 2)
     vmem = pl.BlockSpec(memory_space=pltpu.VMEM)
-    smem = pl.BlockSpec(memory_space=pltpu.SMEM)
-    hbm = pl.BlockSpec(memory_space=pl.ANY)
+    hbm = pl.BlockSpec(memory_space=pltpu.HBM)
     bf16, f32 = jnp.bfloat16, jnp.float32
+    operands = (coarse, reference_frame, data, migration, column_gain.reshape(16, 128), depth_gain.reshape(1, -1))
     scores, moved = pl.pallas_call(
         functools.partial(fused_kernel, slabs, frames),
         out_shape=(
             jax.ShapeDtypeStruct((7, 4, 4, 8), f32),
             jax.ShapeDtypeStruct((3, 4, 4, 8), f32),
         ),
-        in_specs=[smem, smem, hbm, hbm, vmem, vmem, vmem],
+        in_specs=[hbm] * 6,
         out_specs=(vmem, vmem),
         scratch_shapes=[
+            pltpu.SMEM(coarse.shape, jnp.int32),
+            pltpu.SMEM(reference_frame.shape, jnp.int32),
+            pltpu.VMEM(coarse.shape, jnp.int32),
+            pltpu.VMEM((16, 128), f32),
+            pltpu.VMEM((1, depth_gain.shape[0]), f32),
             pltpu.VMEM((elements, depth + 256), bf16),
             pltpu.VMEM(migration.shape, bf16),
             pltpu.VMEM((slabs, 8, 128), bf16),
@@ -437,7 +456,7 @@
             pltpu.VMEM((LX * LY, 128), f32),
             pltpu.VMEM((LX + 2 * MARGIN, LY + 2 * YPAD, 128), f32),
             pltpu.VMEM((16 * 32 * 8, 128), f32),
-            pltpu.SemaphoreType.DMA((3,)),
+            pltpu.SemaphoreType.DMA((8,)),
             pltpu.SemaphoreType.DMA((2,)),
             pltpu.SemaphoreType.DMA((frames - 1,)),
             pltpu.SemaphoreType.DMA((frames - 1,)),
@@ -448,7 +467,7 @@
         compiler_params=pltpu.CompilerParams(
             collective_id=0, has_side_effects=True, vmem_limit_bytes=48 * 2**20
         ),
-    )(coarse, reference_frame, data, migration, column_gain.reshape(16, 128), depth_gain.reshape(1, -1), coarse)
+    )(*[pltpu.with_memory_space_constraint(x, pltpu.HBM) for x in operands])
     return scores.transpose(0, 1, 3, 2)[:, None], moved.transpose(0, 1, 3, 2)[:, None]
 
 

time: 45.9 us -> 39.1 us (0.85)
  local copies, waits for them, and re-layouts: 7.06 us -> 1.23 us
  Pallas kernels: 37.9 us -> 37.2 us
    unnamed x14 -> x2, local copies, waits for them, and re-layouts: 7.06 us -> 1.23 us
    pallas_call x1, Pallas kernels: 37.9 us -> 37.2 us  [per_device(): pl.pallas_call(functools.partial(fused_kernel, slabs, frames), out_shape=...]
where the time goes in v3:
time: 39.1 us; the launch traced here: 39 us
  Pallas kernels  37.2 us (95%)
  local copies, waits for them, and re-layouts  1.23 us (3%)
  between operations  0.64 us (2%)
    pallas_call x1, Pallas kernels, per_device(): pl.pallas_call(functools.partial(fused_kernel, slabs, frames), out_shape=...  37.2 us
    unnamed x2, local copies, waits for them, and re-layouts  1.23 us

profile of v3, /device:TPU:1, one launch (start us, length us, event | category | flops | bytes accessed | tf_op | source)
XLA Modules:
  0.0 39.0 jit_solution(374333108118203853)
XLA Ops:
  0.6 37.2 %shard_map.77 = (f32[7,4,4,8]{3,2,1,0:T(4,128)S(1)}, f32[3,4,4,8]{3,2,1,0:T(4,128)S(1)}) custom-call(s32[3,4,4,8]{3,2,1,0:T(4,128)} %bitcast.19, s32[4]{0:T(128)} %chosen_hbm.1, bf16[16,4096]{1,0:T(8,128)(2,1)} %bitcast.18, bf16[2048,1024]{1,0:T(8,128)(2,1)} %migration_hbm.1, f32[16,128]{1,0:T(8,128)} %bitcast.20, f32[1,64]{1,0:T(1,128)} %bitcast.21), custom_call_target="tpu_custom_call" | custom-call | tf_op jit(solution)/shard_map/pallas_call | solution.py:431
  37.8 0.6 %copy.12 = f32[7,1,4,8,4]{3,4,2,1,0:T(4,128)} copy(f32[7,1,4,8,4]{3,4,2,1,0:T(4,128)S(1)} %bitcast.16) | data formatting | bytes 7168
  38.4 0.6 %copy.13 = f32[3,1,4,8,4]{3,4,2,1,0:T(4,128)} copy(f32[3,1,4,8,4]{3,4,2,1,0:T(4,128)S(1)} %bitcast.17) | data formatting | bytes 3072

commit v4 on v3

--- a/solution.py
+++ b/solution.py
@@ -11,11 +11,13 @@
 KX, KY, KZ = 8, 8, 16
 MARGIN = 9
 YPAD = 16
+YROWS = LY + 2 * YPAD
+PLANES = LX + 2 * MARGIN
 GROUP = 32
 BLOCKS = 4
 EPS = 1e-5
 CELLS = KX * KY * KZ
-ROWS = 256
+ROWS = 1024
 ELEMENTS = 16
 MESH = pl.DeviceIdType.MESH
 
@@ -28,14 +30,16 @@
 
 def clear(volume_ref):
     def one(i, carry):
-        volume_ref[i] = jnp.zeros(volume_ref.shape[1:], volume_ref.dtype)
-        return carry
-
-    lax.fori_loop(0, volume_ref.shape[0], one, 0)
+        rows = pl.ds(pl.multiple_of(i * YROWS, 8), YROWS)
+        volume_ref[rows, :] = jnp.zeros((YROWS, 128), volume_ref.dtype)
+        return carry
+
+    lax.fori_loop(0, PLANES, one, 0)
 
 
 def correlate(image_ref, volume_ref, shift_ref, parts_ref):
     lane = lax.broadcasted_iota(jnp.int32, (8, 128), 1)
+    row = lax.broadcasted_iota(jnp.int32, (8, 128), 0)
     inside = lane % GROUP
     first = lane < GROUP
     third = lane < 3 * GROUP
@@ -47,51 +51,60 @@
     def one(g, carry):
         bx = g // 8
         by = g % 8
-        xs, ys, turns = [], [], []
+        starts, turns = [], []
         for b in range(BLOCKS):
-            xs.append(bx * KX + shift_ref[0, bx, b, by] + MARGIN)
-            ys.append(by * KY + shift_ref[1, bx, b, by] + YPAD)
+            plane = bx * KX + shift_ref[0, bx, b, by] + MARGIN
+            starts.append(plane * YROWS + by * KY + shift_ref[1, bx, b, by] + YPAD)
             turns.append((GROUP * b + 1 - MARGIN - KZ * b + 128 - shift_ref[2, bx, b, by]) % 128)
 
-        def aligned(p, q):
-            turned = [
-                pltpu.roll(volume_ref[xs[b] + p, pl.ds(ys[b] + q, 8), :], turns[b], 1)
-                for b in range(BLOCKS)
-            ]
+        def aligned(rows):
+            turned = [pltpu.roll(volume_ref[rows(starts[b]), :], turns[b], 1) for b in range(BLOCKS)]
             return jnp.where(
                 half,
                 jnp.where(first, turned[0], turned[1]),
                 jnp.where(third, turned[2], turned[3]),
             )
 
-        def kernel_plane(p):
-            row = pl.multiple_of((bx * KX + p) * LY + by * KY, 8)
-            return image_ref[pl.ds(row, 8), :]
+        base = bx * (KX * LY) + by * KY
+
+        def kernel_plane(kind, p):
+            return image_ref[kind, pl.ds(pl.multiple_of(base + p * LY, 8), 8), :]
 
         zero = jnp.zeros((8, 128), jnp.float32)
         cross = [zero] * 7
-        core, xm, xp, ym, yp, own = zero, zero, zero, zero, zero, zero
+        core, own = zero, zero
+        kernels = [kernel_plane(0, p) for p in range(KX)]
         for p in range(-1, KX + 1):
-            window = aligned(p, 0)
+            window = aligned(lambda start: pl.ds(start + p * YROWS, 8))
             power = window * window
-            if 0 <= p < KX:
-                kernel = kernel_plane(p)
-                own = own + kernel * kernel
-                cross[0] += kernel * window
-                cross[5] += pltpu.roll(kernel, 127, 1) * window
-                cross[6] += pltpu.roll(kernel, 1, 1) * window
-                low, high = aligned(p, -1), aligned(p, 1)
-                cross[3] += kernel * low
-                cross[4] += kernel * high
-                ym = ym + low * low
-                yp = yp + high * high
+            if p == -1:
+                ahead = power
+            elif p == KX:
+                behind = power
+            else:
+                own = own + kernels[p] * kernels[p]
+                cross[0] += kernels[p] * window
+                for kind in range(1, 5):
+                    cross[2 + kind] += kernel_plane(kind, p) * window
                 core = core + power
+                if p == 0:
+                    low_end = power
+                if p == KX - 1:
+                    high_end = power
+                if 0 < p < KX - 1:
+                    middle = power if p == 1 else middle + power
             if p < KX - 1:
-                cross[1] += kernel_plane(p + 1) * window
-                xm = xm + power
+                cross[1] += kernels[p + 1] * window
             if p > 0:
-                cross[2] += kernel_plane(p - 1) * window
-                xp = xp + power
+                cross[2] += kernels[p - 1] * window
+        xm = ahead + low_end + middle
+        xp = middle + high_end + behind
+        low = aligned(lambda start: pl.ds(start - 1, KX, stride=YROWS))
+        high = aligned(lambda start: pl.ds(start + KY, KX, stride=YROWS))
+        cross[3] += image_ref[0, pl.ds(base, KX, stride=LY), :] * low
+        cross[4] += image_ref[0, pl.ds(base + KY - 1, KX, stride=LY), :] * high
+        ym = jnp.where(row < KY - 1, core, 0.0) + low * low
+        yp = jnp.where(row > 0, core, 0.0) + high * high
         slots = cross + [own]
         for value, mask in (
             (core, center_mask),
@@ -108,7 +121,7 @@
             parts_ref[pl.ds(pl.multiple_of(k * 256 + g * 8, 8), 8), :] = value
         return carry
 
-    lax.fori_loop(0, 32, one, 0)
+    lax.fori_loop(0, 32, one, 0, unroll=4)
 
 
 def finish(parts_ref, coarse_ref, scores_ref, moved_ref):
@@ -161,7 +174,14 @@
 def make_image(migration_ref, samples_ref, gain_ref, depth_ref, image_ref):
     def one(i, carry):
         rows = pl.ds(pl.multiple_of(i * ROWS, ROWS), ROWS)
-        image_ref[rows, :] = scaled(migration_ref, samples_ref[...], gain_ref, depth_ref[0:1, :], i)
+        image = scaled(migration_ref, samples_ref[...], gain_ref, depth_ref[0:1, :], i)
+        tiles = image.reshape(-1, 8, 128)
+        row = lax.broadcasted_iota(jnp.int32, tiles.shape, 1)
+        image_ref[0, rows, :] = image
+        image_ref[1, rows, :] = jnp.where(row < 7, pltpu.roll(tiles, 7, 1), 0.0).reshape(-1, 128)
+        image_ref[2, rows, :] = jnp.where(row > 0, pltpu.roll(tiles, 1, 1), 0.0).reshape(-1, 128)
+        image_ref[3, rows, :] = pltpu.roll(image, 127, 1)
+        image_ref[4, rows, :] = pltpu.roll(image, 1, 1)
         return carry
 
     lax.fori_loop(0, LX * LY // ROWS, one, 0)
@@ -174,7 +194,8 @@
         samples = samples_ref[...].reshape(-1, 128)
         ref = scaled(migration_ref, samples, gain_ref, depth_ref[1:2, :], i)
         for j in range(planes):
-            volume_ref[MARGIN + i * planes + j, YPAD : YPAD + LY, :] = ref[j * LY : (j + 1) * LY]
+            place = pl.multiple_of((MARGIN + i * planes + j) * YROWS + YPAD, 8)
+            volume_ref[pl.ds(place, LY), :] = ref[j * LY : (j + 1) * LY]
         return carry
 
     lax.fori_loop(0, LX * LY // ROWS, one, 0)
@@ -453,8 +474,8 @@
             pltpu.VMEM((LX * LY, 128), f32),
             pltpu.VMEM((8, 128), f32),
             pltpu.VMEM((slabs * elements, 128), bf16),
-            pltpu.VMEM((LX * LY, 128), f32),
-            pltpu.VMEM((LX + 2 * MARGIN, LY + 2 * YPAD, 128), f32),
+            pltpu.VMEM((5, LX * LY, 128), f32),
+            pltpu.VMEM((PLANES * YROWS, 128), f32),
             pltpu.VMEM((16 * 32 * 8, 128), f32),
             pltpu.SemaphoreType.DMA((8,)),
             pltpu.SemaphoreType.DMA((2,)),

time: 39.1 us -> 33.7 us (0.86)
  Pallas kernels: 37.2 us -> 31.7 us
    pallas_call x1, Pallas kernels: 37.2 us -> 31.7 us  [per_device(): pl.pallas_call(functools.partial(fused_kernel, slabs, frames), out_shape=...]
where the time goes in v4:
time: 33.7 us; the launch traced here: 33.6 us
  Pallas kernels  31.7 us (94%)
  local copies, waits for them, and re-layouts  1.23 us (4%)
  between operations  0.64 us (2%)
    pallas_call x1, Pallas kernels, per_device(): pl.pallas_call(functools.partial(fused_kernel, slabs, frames), out_shape=...  31.7 us
    unnamed x2, local copies, waits for them, and re-layouts  1.23 us

profile of v4, /device:TPU:1, one launch (start us, length us, event | category | flops | bytes accessed | tf_op | source)
XLA Modules:
  0.0 33.6 jit_solution(12227568401452481896)
XLA Ops:
  0.6 31.7 %shard_map.77 = (f32[7,4,4,8]{3,2,1,0:T(4,128)S(1)}, f32[3,4,4,8]{3,2,1,0:T(4,128)S(1)}) custom-call(s32[3,4,4,8]{3,2,1,0:T(4,128)} %bitcast.19, s32[4]{0:T(128)} %chosen_hbm.1, bf16[16,4096]{1,0:T(8,128)(2,1)} %bitcast.18, bf16[2048,1024]{1,0:T(8,128)(2,1)} %migration_hbm.1, f32[16,128]{1,0:T(8,128)} %bitcast.20, f32[1,64]{1,0:T(1,128)} %bitcast.21), custom_call_target="tpu_custom_call" | custom-call | tf_op jit(solution)/shard_map/pallas_call | solution.py:452
  32.3 0.6 %copy.12 = f32[7,1,4,8,4]{3,4,2,1,0:T(4,128)} copy(f32[7,1,4,8,4]{3,4,2,1,0:T(4,128)S(1)} %bitcast.16) | data formatting | bytes 7168
  33.0 0.6 %copy.13 = f32[3,1,4,8,4]{3,4,2,1,0:T(4,128)} copy(f32[3,1,4,8,4]{3,4,2,1,0:T(4,128)S(1)} %bitcast.17) | data formatting | bytes 3072

commit v5 on v4

--- a/solution.py
+++ b/solution.py
@@ -19,6 +19,8 @@
 CELLS = KX * KY * KZ
 ROWS = 1024
 ELEMENTS = 16
+RING = 4
+LINE = 8
 MESH = pl.DeviceIdType.MESH
 
 
@@ -187,12 +189,21 @@
     lax.fori_loop(0, LX * LY // ROWS, one, 0)
 
 
-def make_volume(migration_ref, samples_ref, gain_ref, depth_ref, volume_ref):
+def add_reference(migration_ref, recv_ref, piece, gain_ref, depth_ref, total_ref, volume_ref, first, last):
     planes = ROWS // LY
+    depth = recv_ref[piece].reshape(-1, 128)
+    width = depth.shape[0]
+    columns = pl.ds(pl.multiple_of(piece * width, 128), width)
 
     def one(i, carry):
-        samples = samples_ref[...].reshape(-1, 128)
-        ref = scaled(migration_ref, samples, gain_ref, depth_ref[1:2, :], i)
+        rows = pl.ds(pl.multiple_of(i * ROWS, ROWS), ROWS)
+        raw = jnp.dot(migration_ref[rows, columns], depth, preferred_element_type=jnp.float32)
+        if not first:
+            raw = raw + total_ref[rows, :]
+        if not last:
+            total_ref[rows, :] = raw
+            return carry
+        ref = (raw * gain_ref[rows, :] * depth_ref[1:2, :]).astype(jnp.bfloat16).astype(jnp.float32)
         for j in range(planes):
             place = pl.multiple_of((MARGIN + i * planes + j) * YROWS + YPAD, 8)
             volume_ref[pl.ds(place, LY), :] = ref[j * LY : (j + 1) * LY]
@@ -224,13 +235,13 @@
 
 def pack_own(data_ref, send_ref):
     low = lax.broadcasted_iota(jnp.int32, (8, 128), 1) < 64
-    for t in range(send_ref.shape[0] // 2):
+    for t in range(data_ref.shape[1] // 128 - 2):
         tile = data_ref[:, 128 * (t + 1) : 128 * (t + 2)].astype(jnp.float32)
         first, second = tile[:8], tile[8:]
         even = jnp.where(low, first, pltpu.roll(second, 64, 1))
         odd = jnp.where(low, pltpu.roll(first, 64, 1), second)
-        send_ref[2 * t] = even.astype(jnp.bfloat16)
-        send_ref[2 * t + 1] = odd.astype(jnp.bfloat16)
+        send_ref[2 * t % LINE, 2 * t // LINE] = even.astype(jnp.bfloat16)
+        send_ref[(2 * t + 1) % LINE, 2 * t // LINE] = odd.astype(jnp.bfloat16)
 
 
 def unpack_own(recv_ref, samples_ref):
@@ -257,7 +268,23 @@
             turn = MARGIN + 64 * half
             here, after = parts[m + half], parts[m + half + 1]
             window = jnp.where(lane < turn, pltpu.roll(here, turn, 1), pltpu.roll(after, turn, 1))
-            send_ref[2 * m + half] = window.astype(jnp.bfloat16)
+            place = 2 * m + half
+            send_ref[place % LINE, place // LINE] = window.astype(jnp.bfloat16)
+
+
+def remote(source, target, sems, device):
+    return pltpu.make_async_remote_copy(
+        src_ref=source,
+        dst_ref=target,
+        send_sem=sems.at[0],
+        recv_sem=sems.at[1],
+        device_id=device,
+        device_id_type=MESH,
+    )
+
+
+def wait_bytes(ref, sem):
+    pltpu.make_async_copy(ref, ref, sem).wait()
 
 
 def fused_kernel(
@@ -265,15 +292,32 @@
     shift_hbm, chosen_hbm, data_hbm, migration_hbm, column_hbm, gains_hbm,
     scores_ref, moved_ref,
     shift_ref, chosen_ref, coarse_ref, column_ref, gains_in_ref,
-    data_ref, migration_ref, own_send, own_recv, quarters_ref, ref_send, ref_recv,
-    gains_ref, gain_ref, depth_ref, samples_ref, image_ref, volume_ref, parts_ref,
-    local_sems, own_sems, quarter_send_sems, quarter_recv_sems, ref_sems, gain_send_sems, gain_recv_sems,
+    data_ref, migration_ref, own_send, own_stage, own_recv, quarters_ref, ref_send, ref_stage, ref_recv,
+    gains_ref, gain_ref, depth_ref, samples_ref, image_ref, total_ref, volume_ref, parts_ref,
+    local_sems, quarter_sems, own_line, own_plane, ref_line, ref_plane_send, ref_plane_recv,
+    pair_send, pair_recv, to_next_sems, to_previous_sems,
 ):
     frame = lax.axis_index("frame")
     slab = lax.axis_index("slab")
-    share = slabs // frames
-    source = slab // share
-    same = jnp.where(source == frame, 1, 0)
+    column, depth_place = slab // LINE, slab % LINE
+    columns = slabs // LINE
+    place_x, place_y, core = column // 2, column % 2, frame % 2
+    other_core = frame + 1 - 2 * core
+    def distance(of_frame):
+        return jnp.where(of_frame == 0, 1, jnp.where(of_frame == 1, 3, jnp.where(of_frame == 2, 0, 2)))
+
+    frame_at = (2, 0, 3, 1)
+    target_x = (place_x + distance(frame)) % RING
+    keeps = (target_x == place_x) & (core == place_y)
+    has_next = slab < slabs - 1
+    has_previous = slab > 0
+    next_slab, previous_slab = (slab + 1) % slabs, (slab + slabs - 1) % slabs
+
+    def on_line(i):
+        return {"frame": frame, "slab": column * LINE + (depth_place + i) % LINE}
+
+    def on_plane(i):
+        return {"frame": frame, "slab": (column + i) % columns * LINE + depth_place}
 
     width = data_hbm.shape[1]
     loads = [
@@ -293,152 +337,147 @@
     for copy in loads:
         copy.start()
     gains_ref[...] = jnp.zeros(gains_ref.shape, gains_ref.dtype)
+
     barrier = pltpu.get_barrier_semaphore()
 
-    def greet(target_frame, target_slab):
-        pl.semaphore_signal(
-            barrier, inc=1, device_id={"frame": target_frame, "slab": target_slab}, device_id_type=MESH
-        )
-
-    def greet_own(i, carry):
-        greet(frame, (slab + 1 + i) % slabs)
-        return carry
-
-    def greet_source(i, carry):
-        other = (slab + i) % slabs
-
-        @pl.when((other != slab) | (source != frame))
-        def _():
-            greet(source, other)
-
-        return carry
-
+    def greet(device):
+        pl.semaphore_signal(barrier, inc=1, device_id=device, device_id_type=MESH)
+
+    for i in range(1, LINE):
+        greet(on_line(i))
+    for i in range(1, columns):
+        greet(on_plane(i))
+    for i in range(RING):
+        x = (place_x + i) % RING
+        device = {"frame": frame_at[-i % RING], "slab": (x * 2 + core) * LINE + depth_place}
+        if i == 0:
+            pl.when(jnp.logical_not(keeps))(functools.partial(greet, device))
+        else:
+            greet(device)
     for i in range(1, frames):
-        greet((frame + i) % frames, slab)
-    lax.fori_loop(0, slabs - 1, greet_own, 0)
-    lax.fori_loop(0, slabs, greet_source, 0)
+        greet({"frame": (frame + i) % frames, "slab": slab})
+    pl.when(has_next)(lambda: greet({"frame": frame, "slab": next_slab}))
+    pl.when(has_previous)(lambda: greet({"frame": frame, "slab": previous_slab}))
 
     data_ref[:, :128] = jnp.zeros((ELEMENTS, 128), data_ref.dtype)
     data_ref[:, -128:] = jnp.zeros((ELEMENTS, 128), data_ref.dtype)
     for copy in loads[:3]:
         copy.wait()
     gains_ref[1, :, :64] = gains_in_ref[...]
-    pl.semaphore_wait(barrier, (frames - 1) + (slabs - 1) + slabs - same)
+    pack_own(data_ref, own_send)
+    greetings = (LINE - 1) + (columns - 1) + 4 - jnp.where(keeps, 1, 0) + (frames - 1)
+    greetings = greetings + jnp.where(has_next, 1, 0) + jnp.where(has_previous, 1, 0)
+    pl.semaphore_wait(barrier, greetings)
 
     quarter = width // frames
 
-    def quarter_of(i):
-        return data_ref.at[:, pl.ds(pl.multiple_of(i * quarter, 128), quarter + 256)]
-
-    quarter_copies = []
+    def quarter_of(of_frame):
+        place = (place_x + distance(of_frame)) % RING
+        return data_ref.at[:, pl.ds(pl.multiple_of(place * quarter, 128), quarter + 256)]
+
     for i in range(1, frames):
         other = (frame + i) % frames
+        remote(
+            quarter_of(other), quarters_ref.at[frame], quarter_sems, {"frame": other, "slab": slab}
+        ).start()
+    pltpu.make_async_copy(quarter_of(frame), quarters_ref.at[frame], quarter_sems.at[1]).start()
+
+    def along_line(send_ref, stage_ref, sems):
+        for i in (4, 3, 5, 2, 6, 1, 7):
+            there = (depth_place + i) % LINE
+            remote(send_ref.at[there], stage_ref.at[depth_place], sems, on_line(i)).start()
+        pltpu.make_async_copy(send_ref.at[depth_place], stage_ref.at[depth_place], sems.at[1]).start()
+
+    along_line(own_send, own_stage, own_line)
+
+    to_next = remote(gains_ref.at[1], gains_ref.at[0], to_next_sems, {"frame": frame, "slab": next_slab})
+    to_previous = remote(
+        gains_ref.at[1], gains_ref.at[2], to_previous_sems, {"frame": frame, "slab": previous_slab}
+    )
+    pl.when(has_next)(to_next.start)
+    pl.when(has_previous)(to_previous.start)
+
+    wait_bytes(quarters_ref, quarter_sems.at[1])
+    pack_reference(quarters_ref, chosen_ref[0], ref_send)
+    along_line(ref_send, ref_stage, ref_line)
+
+    for copy in loads[3:]:
+        copy.wait()
+    clear(volume_ref)
+
+    here = pl.ds(column * LINE, LINE)
+    wait_bytes(own_stage, own_line.at[1])
+    for i in range(1, columns):
+        there = (column + i) % columns
+        remote(own_stage.at[:, there], own_recv.at[here], own_plane, on_plane(i)).start()
+    pltpu.make_async_copy(own_stage.at[:, column], own_recv.at[here], own_plane.at[1]).start()
+    expand_gain(column_ref, gain_ref)
+
+    wait_bytes(ref_stage, ref_line.at[1])
+    for a, b in ((1, 1), (1, 0), (0, 1), (0, 0)):
+        to_y = (place_y + a) % 2
+        to_frame = (frame // 2 + b) % 2 * 2 + place_y
         copy = pltpu.make_async_remote_copy(
-            src_ref=quarter_of(other),
-            dst_ref=quarters_ref.at[frame],
-            send_sem=quarter_send_sems.at[i - 1],
-            recv_sem=quarter_recv_sems.at[i - 1],
-            device_id={"frame": other},
+            src_ref=ref_stage.at[:, to_y],
+            dst_ref=ref_recv.at[place_x, place_y],
+            send_sem=ref_plane_send.at[0],
+            recv_sem=ref_plane_recv.at[place_x],
+            device_id={"frame": to_frame, "slab": (target_x * 2 + to_y) * LINE + depth_place},
             device_id_type=MESH,
         )
-        copy.start()
-        quarter_copies.append(copy)
-    keep_quarter = pltpu.make_async_copy(quarter_of(frame), quarters_ref.at[frame], local_sems.at[7])
-    keep_quarter.start()
-
-    pack_own(data_ref, own_send)
-
-    def send_own(i, carry):
-        other = (slab + 1 + i) % slabs
-        pltpu.make_async_remote_copy(
-            src_ref=own_send.at[other],
-            dst_ref=own_recv.at[slab],
-            send_sem=own_sems.at[0],
-            recv_sem=own_sems.at[1],
-            device_id={"slab": other},
-            device_id_type=MESH,
+        if a == 0 and b == 0:
+            pl.when(jnp.logical_not(keeps))(copy.start)
+        else:
+            copy.start()
+
+    @pl.when(keeps)
+    def _():
+        pltpu.make_async_copy(
+            ref_stage.at[:, place_y], ref_recv.at[place_x, place_y], ref_plane_recv.at[place_x]
         ).start()
-        return carry
-
-    lax.fori_loop(0, slabs - 1, send_own, 0)
-    pltpu.make_async_copy(own_send.at[slab], own_recv.at[slab], own_sems.at[1]).start()
-
-    def gain_copy(way, other):
-        return pltpu.make_async_remote_copy(
-            src_ref=gains_ref.at[1],
-            dst_ref=gains_ref.at[1 - way],
-            send_sem=gain_send_sems.at[max(way, 0)],
-            recv_sem=gain_recv_sems.at[max(way, 0)],
-            device_id={"slab": other},
-            device_id_type=MESH,
-        )
-
-    to_next = gain_copy(1, (slab + 1) % slabs)
-    to_previous = gain_copy(-1, (slab + slabs - 1) % slabs)
-    has_next = slab < slabs - 1
-    has_previous = slab > 0
-    pl.when(has_next)(to_next.start)
-    pl.when(has_previous)(to_previous.start)
-
-    for copy in quarter_copies:
-        copy.wait_recv()
-    keep_quarter.wait()
-    pack_reference(quarters_ref, chosen_ref[0], ref_send)
-
-    def send_reference(i, carry):
-        place = (slab + i // frames) % share
-        to_frame = (frame + i) % frames
-        to_slab = frame * share + place
-        here = (to_frame == frame) & (to_slab == slab)
-
-        @pl.when(jnp.logical_not(here))
-        def _():
-            pltpu.make_async_remote_copy(
-                src_ref=ref_send.at[place],
-                dst_ref=ref_recv.at[slab],
-                send_sem=ref_sems.at[0],
-                recv_sem=ref_sems.at[1],
-                device_id={"frame": to_frame, "slab": to_slab},
-                device_id_type=MESH,
-            ).start()
-
-        return carry
-
-    lax.fori_loop(0, slabs, send_reference, 0)
-
-    @pl.when(source == frame)
-    def _():
-        pltpu.make_async_copy(ref_send.at[slab % share], ref_recv.at[slab], ref_sems.at[1]).start()
-
-    for copy in loads[3:]:
-        copy.wait()
-    expand_gain(column_ref, gain_ref)
-    clear(volume_ref)
+
     pl.when(has_previous)(to_next.wait_recv)
     pl.when(has_next)(to_previous.wait_recv)
     spread_depth(gains_ref, depth_ref)
-    pltpu.make_async_copy(own_recv, own_recv, own_sems.at[1]).wait()
+    wait_bytes(own_recv, own_plane.at[1])
     unpack_own(own_recv, samples_ref)
     make_image(migration_ref, samples_ref, gain_ref, depth_ref, image_ref)
-    pltpu.make_async_copy(ref_recv, ref_recv, ref_sems.at[1]).wait()
-    make_volume(migration_ref, ref_recv, gain_ref, depth_ref, volume_ref)
+    pieces = [(place_x + i) % RING for i in (0, 1, 3, 2)]
+    for x in pieces:
+        copy = pltpu.make_async_remote_copy(
+            src_ref=ref_recv.at[x, core],
+            dst_ref=ref_recv.at[x, core],
+            send_sem=pair_send.at[0],
+            recv_sem=pair_recv.at[x],
+            device_id={"frame": other_core, "slab": slab},
+            device_id_type=MESH,
+        )
+        wait_bytes(ref_recv.at[x, core], ref_plane_recv.at[x])
+        copy.start()
+    for i, x in enumerate(pieces):
+        wait_bytes(ref_recv.at[x, 1 - core], pair_recv.at[x])
+        add_reference(
+            migration_ref, ref_recv, x, gain_ref, depth_ref, total_ref, volume_ref, i == 0, i == RING - 1
+        )
     correlate(image_ref, volume_ref, shift_ref, parts_ref)
     finish(parts_ref, coarse_ref, scores_ref, moved_ref)
 
-    for copy in quarter_copies:
-        copy.wait_send()
     pl.when(has_next)(to_next.wait_send)
     pl.when(has_previous)(to_previous.wait_send)
-    most = pl.ds(0, slabs - 1)
-    pltpu.make_async_copy(own_recv.at[most], own_recv.at[most], own_sems.at[0]).wait()
-
-    @pl.when(source == frame)
+    wait_bytes(quarters_ref.at[pl.ds(0, frames - 1)], quarter_sems.at[0])
+    wait_bytes(own_stage.at[pl.ds(0, LINE - 1)], own_line.at[0])
+    wait_bytes(ref_stage.at[pl.ds(0, LINE - 1)], ref_line.at[0])
+    wait_bytes(own_recv.at[pl.ds(0, slabs - LINE)], own_plane.at[0])
+
+    wait_bytes(own_recv, pair_send.at[0])
+
+    @pl.when(keeps)
     def _():
-        pltpu.make_async_copy(ref_recv.at[most], ref_recv.at[most], ref_sems.at[0]).wait()
-
-    @pl.when(source != frame)
+        wait_bytes(own_recv.at[pl.ds(0, slabs // 4 * 3)], ref_plane_send.at[0])
+
+    @pl.when(jnp.logical_not(keeps))
     def _():
-        pltpu.make_async_copy(ref_recv, ref_recv, ref_sems.at[0]).wait()
+        wait_bytes(own_recv, ref_plane_send.at[0])
 
 
 def per_device(slabs, frames, element_data, migration, column_gain, depth_gain, coarse_shift, reference_frame):
@@ -465,23 +504,30 @@
             pltpu.VMEM((1, depth_gain.shape[0]), f32),
             pltpu.VMEM((elements, depth + 256), bf16),
             pltpu.VMEM(migration.shape, bf16),
-            pltpu.VMEM((slabs, 8, 128), bf16),
+            pltpu.VMEM((LINE, slabs // LINE, 8, 128), bf16),
+            pltpu.VMEM((LINE, slabs // LINE, 8, 128), bf16),
             pltpu.VMEM((slabs, 8, 128), bf16),
             pltpu.VMEM((frames, elements, depth // frames + 256), bf16),
-            pltpu.VMEM((slabs // frames, elements, 128), bf16),
-            pltpu.VMEM((slabs, elements, 128), bf16),
+            pltpu.VMEM((LINE, slabs // frames // LINE, elements, 128), bf16),
+            pltpu.VMEM((LINE, slabs // frames // LINE, elements, 128), bf16),
+            pltpu.VMEM((RING, 2, LINE, elements, 128), bf16),
             pltpu.VMEM((3, 1, 128), f32),
             pltpu.VMEM((LX * LY, 128), f32),
             pltpu.VMEM((8, 128), f32),
             pltpu.VMEM((slabs * elements, 128), bf16),
             pltpu.VMEM((5, LX * LY, 128), f32),
+            pltpu.VMEM((LX * LY, 128), f32),
             pltpu.VMEM((PLANES * YROWS, 128), f32),
             pltpu.VMEM((16 * 32 * 8, 128), f32),
-            pltpu.SemaphoreType.DMA((8,)),
+            pltpu.SemaphoreType.DMA((7,)),
             pltpu.SemaphoreType.DMA((2,)),
-            pltpu.SemaphoreType.DMA((frames - 1,)),
-            pltpu.SemaphoreType.DMA((frames - 1,)),
             pltpu.SemaphoreType.DMA((2,)),
+            pltpu.SemaphoreType.DMA((2,)),
+            pltpu.SemaphoreType.DMA((2,)),
+            pltpu.SemaphoreType.DMA((1,)),
+            pltpu.SemaphoreType.DMA((RING,)),
+            pltpu.SemaphoreType.DMA((1,)),
+            pltpu.SemaphoreType.DMA((RING,)),
             pltpu.SemaphoreType.DMA((2,)),
             pltpu.SemaphoreType.DMA((2,)),
         ],

time: 33.7 us -> 32.4 us (0.961)
  Pallas kernels: 31.7 us -> 30.4 us
    pallas_call x1, Pallas kernels: 31.7 us -> 30.4 us  [per_device(): pl.pallas_call(functools.partial(fused_kernel, slabs, frames), out_shape=...]
where the time goes in v5:
time: 32.4 us; the launch traced here: 32.3 us
  Pallas kernels  30.4 us (94%)
  local copies, waits for them, and re-layouts  1.23 us (4%)
  between operations  0.64 us (2%)
    pallas_call x1, Pallas kernels, per_device(): pl.pallas_call(functools.partial(fused_kernel, slabs, frames), out_shape=...  30.4 us
    unnamed x2, local copies, waits for them, and re-layouts  1.23 us

profile of v5, /device:TPU:1, one launch (start us, length us, event | category | flops | bytes accessed | tf_op | source)
XLA Modules:
  0.0 32.3 jit_solution(16970818169040285833)
XLA Ops:
  0.6 30.4 %shard_map.77 = (f32[7,4,4,8]{3,2,1,0:T(4,128)S(1)}, f32[3,4,4,8]{3,2,1,0:T(4,128)S(1)}) custom-call(s32[3,4,4,8]{3,2,1,0:T(4,128)} %bitcast.19, s32[4]{0:T(128)} %chosen_hbm.1, bf16[16,4096]{1,0:T(8,128)(2,1)} %bitcast.18, bf16[2048,1024]{1,0:T(8,128)(2,1)} %migration_hbm.1, f32[16,128]{1,0:T(8,128)} %bitcast.20, f32[1,64]{1,0:T(1,128)} %bitcast.21), custom_call_target="tpu_custom_call" | custom-call | tf_op jit(solution)/shard_map/pallas_call | solution.py:491
  31.1 0.6 %copy.12 = f32[7,1,4,8,4]{3,4,2,1,0:T(4,128)} copy(f32[7,1,4,8,4]{3,4,2,1,0:T(4,128)S(1)} %bitcast.16) | data formatting | bytes 7168
  31.7 0.6 %copy.13 = f32[3,1,4,8,4]{3,4,2,1,0:T(4,128)} copy(f32[3,1,4,8,4]{3,4,2,1,0:T(4,128)S(1)} %bitcast.17) | data formatting | bytes 3072

commit v6 on v5

--- a/solution.py
+++ b/solution.py
@@ -21,6 +21,7 @@
 ELEMENTS = 16
 RING = 4
 LINE = 8
+SEVERAL = 4
 MESH = pl.DeviceIdType.MESH
 
 
@@ -39,7 +40,7 @@
     lax.fori_loop(0, PLANES, one, 0)
 
 
-def correlate(image_ref, volume_ref, shift_ref, parts_ref):
+def correlate(image_ref, volume_ref, shift_ref, parts_ref, begin, end, beside=None):
     lane = lax.broadcasted_iota(jnp.int32, (8, 128), 1)
     row = lax.broadcasted_iota(jnp.int32, (8, 128), 0)
     inside = lane % GROUP
@@ -123,7 +124,14 @@
             parts_ref[pl.ds(pl.multiple_of(k * 256 + g * 8, 8), 8), :] = value
         return carry
 
-    lax.fori_loop(0, 32, one, 0, unroll=4)
+    def several(i, carry):
+        if beside is not None:
+            beside(i - begin // SEVERAL)
+        for j in range(SEVERAL):
+            one(i * SEVERAL + j, carry)
+        return carry
+
+    lax.fori_loop(begin // SEVERAL, end // SEVERAL, several, 0)
 
 
 def finish(parts_ref, coarse_ref, scores_ref, moved_ref):
@@ -132,13 +140,18 @@
         total = total + parts_ref[pl.ds(s, 512, stride=8), :]
     picked = lax.broadcasted_iota(jnp.int32, (8, 128), 1) // GROUP
     picked = (picked == lax.broadcasted_iota(jnp.int32, (8, 128), 0)).astype(jnp.float32)
-    sums = lax.dot_general(
-        picked,
-        total,
-        (((1,), (1,)), ((), ())),
-        precision=lax.Precision.HIGHEST,
-        preferred_element_type=jnp.float32,
-    ) * (1.0 / CELLS)
+    high = total.astype(jnp.bfloat16)
+    low = (total - high.astype(jnp.float32)).astype(jnp.bfloat16)
+    sums = [
+        lax.dot_general(
+            picked.astype(jnp.bfloat16),
+            part,
+            (((1,), (1,)), ((), ())),
+            preferred_element_type=jnp.float32,
+        )
+        for part in (high, low)
+    ]
+    sums = (sums[0] + sums[1]) * (1.0 / CELLS)
     tiles = [sums[:, 128 * i : 128 * (i + 1)] for i in range(4)]
     lane = lax.broadcasted_iota(jnp.int32, (8, 128), 1)
     own = jnp.where(lane >= 3 * GROUP, tiles[3], 0.0)
@@ -189,27 +202,17 @@
     lax.fori_loop(0, LX * LY // ROWS, one, 0)
 
 
-def add_reference(migration_ref, recv_ref, piece, gain_ref, depth_ref, total_ref, volume_ref, first, last):
-    planes = ROWS // LY
-    depth = recv_ref[piece].reshape(-1, 128)
-    width = depth.shape[0]
-    columns = pl.ds(pl.multiple_of(piece * width, 128), width)
-
-    def one(i, carry):
-        rows = pl.ds(pl.multiple_of(i * ROWS, ROWS), ROWS)
-        raw = jnp.dot(migration_ref[rows, columns], depth, preferred_element_type=jnp.float32)
-        if not first:
-            raw = raw + total_ref[rows, :]
-        if not last:
-            total_ref[rows, :] = raw
-            return carry
-        ref = (raw * gain_ref[rows, :] * depth_ref[1:2, :]).astype(jnp.bfloat16).astype(jnp.float32)
-        for j in range(planes):
-            place = pl.multiple_of((MARGIN + i * planes + j) * YROWS + YPAD, 8)
-            volume_ref[pl.ds(place, LY), :] = ref[j * LY : (j + 1) * LY]
-        return carry
-
-    lax.fori_loop(0, LX * LY // ROWS, one, 0)
+def reference_raw(migration_ref, recv_ref, total_ref, start, count):
+    samples = recv_ref[...].reshape(-1, 128)
+    rows = pl.ds(start, count)
+    total_ref[rows, :] = jnp.dot(migration_ref[rows, :], samples, preferred_element_type=jnp.float32)
+
+
+def reference_planes(total_ref, gain_ref, depth_ref, volume_ref, start, count):
+    for plane in range(start, start + count):
+        rows = pl.ds(plane * LY, LY)
+        ref = (total_ref[rows, :] * gain_ref[rows, :] * depth_ref[1:2, :]).astype(jnp.bfloat16)
+        volume_ref[pl.ds((MARGIN + plane) * YROWS + YPAD, LY), :] = ref.astype(jnp.float32)
 
 
 def place_of(column):
@@ -454,12 +457,24 @@
         )
         wait_bytes(ref_recv.at[x, core], ref_plane_recv.at[x])
         copy.start()
-    for i, x in enumerate(pieces):
+    for x in pieces:
         wait_bytes(ref_recv.at[x, 1 - core], pair_recv.at[x])
-        add_reference(
-            migration_ref, ref_recv, x, gain_ref, depth_ref, total_ref, volume_ref, i == 0, i == RING - 1
-        )
-    correlate(image_ref, volume_ref, shift_ref, parts_ref)
+    reach = 2 * KX + 1
+    reference_raw(migration_ref, ref_recv, total_ref, 0, reach * LY)
+    reference_planes(total_ref, gain_ref, depth_ref, volume_ref, 0, reach)
+    for bx in range(LX // KX):
+        planes = min(KX, LX - reach)
+        beside = None
+        if planes:
+            count = planes * LY * SEVERAL // 8
+
+            def beside(i, reach=reach, count=count):
+                start = pl.multiple_of(reach * LY + i * count, 32)
+                reference_raw(migration_ref, ref_recv, total_ref, start, count)
+
+        correlate(image_ref, volume_ref, shift_ref, parts_ref, bx * 8, bx * 8 + 8, beside)
+        reference_planes(total_ref, gain_ref, depth_ref, volume_ref, reach, planes)
+        reach += planes
     finish(parts_ref, coarse_ref, scores_ref, moved_ref)
 
     pl.when(has_next)(to_next.wait_send)

time: 32.4 us -> 30.9 us (0.954)
  Pallas kernels: 30.4 us -> 29 us
    pallas_call x1, Pallas kernels: 30.4 us -> 29 us  [per_device(): pl.pallas_call(functools.partial(fused_kernel, slabs, frames), out_shape=...]
where the time goes in v6:
time: 30.9 us; the launch traced here: 30.8 us
  Pallas kernels  29 us (94%)
  local copies, waits for them, and re-layouts  1.23 us (4%)
  between operations  0.64 us (2%)
    pallas_call x1, Pallas kernels, per_device(): pl.pallas_call(functools.partial(fused_kernel, slabs, frames), out_shape=...  29 us
    unnamed x2, local copies, waits for them, and re-layouts  1.23 us

profile of v6, /device:TPU:1, one launch (start us, length us, event | category | flops | bytes accessed | tf_op | source)
XLA Modules:
  0.0 30.8 jit_solution(15205949045525801061)
XLA Ops:
  0.6 29.0 %shard_map.77 = (f32[7,4,4,8]{3,2,1,0:T(4,128)S(1)}, f32[3,4,4,8]{3,2,1,0:T(4,128)S(1)}) custom-call(s32[3,4,4,8]{3,2,1,0:T(4,128)} %bitcast.19, s32[4]{0:T(128)} %chosen_hbm.1, bf16[16,4096]{1,0:T(8,128)(2,1)} %bitcast.18, bf16[2048,1024]{1,0:T(8,128)(2,1)} %migration_hbm.1, f32[16,128]{1,0:T(8,128)} %bitcast.20, f32[1,64]{1,0:T(1,128)} %bitcast.21), custom_call_target="tpu_custom_call" | custom-call | tf_op jit(solution)/shard_map/pallas_call | solution.py:506
  29.6 0.6 %copy.12 = f32[7,1,4,8,4]{3,4,2,1,0:T(4,128)} copy(f32[7,1,4,8,4]{3,4,2,1,0:T(4,128)S(1)} %bitcast.16) | data formatting | bytes 7168
  30.2 0.6 %copy.13 = f32[3,1,4,8,4]{3,4,2,1,0:T(4,128)} copy(f32[3,1,4,8,4]{3,4,2,1,0:T(4,128)S(1)} %bitcast.17) | data formatting | bytes 3072

commit v7 on v6

--- a/solution.py
+++ b/solution.py
@@ -293,10 +293,10 @@
 def fused_kernel(
     slabs, frames,
     shift_hbm, chosen_hbm, data_hbm, migration_hbm, column_hbm, gains_hbm,
-    scores_ref, moved_ref,
-    shift_ref, chosen_ref, coarse_ref, column_ref, gains_in_ref,
+    parts_ref,
+    shift_ref, chosen_ref, column_ref, gains_in_ref,
     data_ref, migration_ref, own_send, own_stage, own_recv, quarters_ref, ref_send, ref_stage, ref_recv,
-    gains_ref, gain_ref, depth_ref, samples_ref, image_ref, total_ref, volume_ref, parts_ref,
+    gains_ref, gain_ref, depth_ref, samples_ref, image_ref, total_ref, volume_ref,
     local_sems, quarter_sems, own_line, own_plane, ref_line, ref_plane_send, ref_plane_recv,
     pair_send, pair_recv, to_next_sems, to_previous_sems,
 ):
@@ -333,7 +333,6 @@
                 (migration_hbm, migration_ref),
                 (column_hbm, column_ref),
                 (shift_hbm, shift_ref),
-                (shift_hbm, coarse_ref),
             )
         )
     ]
@@ -475,7 +474,6 @@
         correlate(image_ref, volume_ref, shift_ref, parts_ref, bx * 8, bx * 8 + 8, beside)
         reference_planes(total_ref, gain_ref, depth_ref, volume_ref, reach, planes)
         reach += planes
-    finish(parts_ref, coarse_ref, scores_ref, moved_ref)
 
     pl.when(has_next)(to_next.wait_send)
     pl.when(has_previous)(to_previous.wait_send)
@@ -503,18 +501,14 @@
     hbm = pl.BlockSpec(memory_space=pltpu.HBM)
     bf16, f32 = jnp.bfloat16, jnp.float32
     operands = (coarse, reference_frame, data, migration, column_gain.reshape(16, 128), depth_gain.reshape(1, -1))
-    scores, moved = pl.pallas_call(
+    parts = pl.pallas_call(
         functools.partial(fused_kernel, slabs, frames),
-        out_shape=(
-            jax.ShapeDtypeStruct((7, 4, 4, 8), f32),
-            jax.ShapeDtypeStruct((3, 4, 4, 8), f32),
-        ),
+        out_shape=jax.ShapeDtypeStruct((16 * 32 * 8, 128), f32),
         in_specs=[hbm] * 6,
-        out_specs=(vmem, vmem),
+        out_specs=vmem,
         scratch_shapes=[
             pltpu.SMEM(coarse.shape, jnp.int32),
             pltpu.SMEM(reference_frame.shape, jnp.int32),
-            pltpu.VMEM(coarse.shape, jnp.int32),
             pltpu.VMEM((16, 128), f32),
             pltpu.VMEM((1, depth_gain.shape[0]), f32),
             pltpu.VMEM((elements, depth + 256), bf16),
@@ -533,8 +527,7 @@
             pltpu.VMEM((5, LX * LY, 128), f32),
             pltpu.VMEM((LX * LY, 128), f32),
             pltpu.VMEM((PLANES * YROWS, 128), f32),
-            pltpu.VMEM((16 * 32 * 8, 128), f32),
-            pltpu.SemaphoreType.DMA((7,)),
+            pltpu.SemaphoreType.DMA((6,)),
             pltpu.SemaphoreType.DMA((2,)),
             pltpu.SemaphoreType.DMA((2,)),
             pltpu.SemaphoreType.DMA((2,)),
@@ -550,6 +543,16 @@
             collective_id=0, has_side_effects=True, vmem_limit_bytes=48 * 2**20
         ),
     )(*[pltpu.with_memory_space_constraint(x, pltpu.HBM) for x in operands])
+    scores, moved = pl.pallas_call(
+        finish,
+        out_shape=(
+            jax.ShapeDtypeStruct((7, 4, 4, 8), f32),
+            jax.ShapeDtypeStruct((3, 4, 4, 8), f32),
+        ),
+        in_specs=[vmem, vmem],
+        out_specs=(vmem, vmem),
+        compiler_params=pltpu.CompilerParams(vmem_limit_bytes=8 * 2**20),
+    )(parts, coarse)
     return scores.transpose(0, 1, 3, 2)[:, None], moved.transpose(0, 1, 3, 2)[:, None]
 
 

time: 30.9 us -> 30.3 us (0.981)
  local copies, waits for them, and re-layouts: 1.23 us -> 0.01 us
  Pallas kernels: 29 us -> 29.6 us
    pallas_call x0 -> x1, Pallas kernels: none -> 1.24 us  [per_device(): pl.pallas_call(finish, out_shape=(jax.ShapeDtypeStruct((7, 4, 4, 8), f32)...]
    unnamed x2, local copies, waits for them, and re-layouts: 1.23 us -> 0.01 us
    pallas_call x1, Pallas kernels: 29 us -> 28.3 us  [per_device(): pl.pallas_call(functools.partial(fused_kernel, slabs, frames), out_shape=...]
where the time goes in v7:
time: 30.3 us; the launch traced here: 30.2 us
  Pallas kernels  29.6 us (98%)
  between operations  0.66 us (2%)
    pallas_call x1, Pallas kernels, per_device(): pl.pallas_call(functools.partial(fused_kernel, slabs, frames), out_shape=...  28.3 us
    pallas_call x1, Pallas kernels, per_device(): pl.pallas_call(finish, out_shape=(jax.ShapeDtypeStruct((7, 4, 4, 8), f32)...  1.24 us

profile of v7, /device:TPU:1, one launch (start us, length us, event | category | flops | bytes accessed | tf_op | source)
XLA Modules:
  0.0 30.2 jit_solution(10186420984938736560)
XLA Ops:
  0.6 0.0 copy-start
  0.6 28.3 %shard_map.77.parts_ref = f32[4096,128]{1,0:T(8,128)S(1)} custom-call(s32[3,4,4,8]{3,2,1,0:T(4,128)} %bitcast.16, s32[4]{0:T(128)} %chosen_hbm.1, bf16[16,4096]{1,0:T(8,128)(2,1)} %bitcast.18, bf16[2048,1024]{1,0:T(8,128)(2,1)} %migration_hbm.1, f32[16,128]{1,0:T(8,128)} %bitcast.19, f32[1,64]{1,0:T(1,128)} %bitcast.20), custom_call_target="tpu_custom_call" | custom-call | tf_op jit(solution)/shard_map/pallas_call | solution.py:504
  29.0 0.0 copy-done
  29.0 1.2 %shard_map.78 = (f32[7,4,4,8]{3,2,1,0:T(4,128)}, f32[3,4,4,8]{3,2,1,0:T(4,128)}) custom-call(f32[4096,128]{1,0:T(8,128)S(1)} %shard_map.77.parts_ref, s32[3,4,4,8]{3,2,1,0:T(4,128)S(1)} %bitcast.17), custom_call_target="tpu_custom_call" | custom-call | tf_op jit(solution)/shard_map/pallas_call | solution.py:546
Async XLA Ops:
  0.6 28.3 %copy-start = (s32[3,1,4,8,4]{3,4,2,1,0:T(4,128)S(1)}, s32[3,1,4,8,4]{3,4,2,1,0:T(4,128)}, u32[]{:S(2)}) copy-start(s32[3,1,4,8,4]{3,4,2,1,0:T(4,128)} %param.10) | copy-start | bytes 4612

commit v8 on v7

--- a/solution.py
+++ b/solution.py
@@ -471,6 +471,9 @@
                 start = pl.multiple_of(reach * LY + i * count, 32)
                 reference_raw(migration_ref, ref_recv, total_ref, start, count)
 
+        if beside is None:
+            correlate(image_ref, volume_ref, shift_ref, parts_ref, bx * 8, 32)
+            break
         correlate(image_ref, volume_ref, shift_ref, parts_ref, bx * 8, bx * 8 + 8, beside)
         reference_planes(total_ref, gain_ref, depth_ref, volume_ref, reach, planes)
         reach += planes

time: 30.3 us -> 30.3 us (level)
  no operation moved by 1% of the time
where the time goes in v8:
time: 30.3 us; the launch traced here: 30.2 us
  Pallas kernels  29.6 us (98%)
  between operations  0.66 us (2%)
    pallas_call x1, Pallas kernels, per_device(): pl.pallas_call(functools.partial(fused_kernel, slabs, frames), out_shape=...  28.3 us
    pallas_call x1, Pallas kernels, per_device(): pl.pallas_call(finish, out_shape=(jax.ShapeDtypeStruct((7, 4, 4, 8), f32)...  1.24 us

profile of v8, /device:TPU:1, one launch (start us, length us, event | category | flops | bytes accessed | tf_op | source)
XLA Modules:
  0.0 30.2 jit_solution(8668414922587130326)
XLA Ops:
  0.6 0.0 copy-start
  0.6 28.3 %shard_map.77.parts_ref = f32[4096,128]{1,0:T(8,128)S(1)} custom-call(s32[3,4,4,8]{3,2,1,0:T(4,128)} %bitcast.16, s32[4]{0:T(128)} %chosen_hbm.1, bf16[16,4096]{1,0:T(8,128)(2,1)} %bitcast.18, bf16[2048,1024]{1,0:T(8,128)(2,1)} %migration_hbm.1, f32[16,128]{1,0:T(8,128)} %bitcast.19, f32[1,64]{1,0:T(1,128)} %bitcast.20), custom_call_target="tpu_custom_call" | custom-call | tf_op jit(solution)/shard_map/pallas_call | solution.py:507
  29.0 0.0 copy-done
  29.0 1.2 %shard_map.78 = (f32[7,4,4,8]{3,2,1,0:T(4,128)}, f32[3,4,4,8]{3,2,1,0:T(4,128)}) custom-call(f32[4096,128]{1,0:T(8,128)S(1)} %shard_map.77.parts_ref, s32[3,4,4,8]{3,2,1,0:T(4,128)S(1)} %bitcast.17), custom_call_target="tpu_custom_call" | custom-call | tf_op jit(solution)/shard_map/pallas_call | solution.py:549
Async XLA Ops:
  0.6 28.4 %copy-start = (s32[3,1,4,8,4]{3,4,2,1,0:T(4,128)S(1)}, s32[3,1,4,8,4]{3,4,2,1,0:T(4,128)}, u32[]{:S(2)}) copy-start(s32[3,1,4,8,4]{3,4,2,1,0:T(4,128)} %param.10) | copy-start | bytes 4612

commit v9 on v8

--- a/solution.py
+++ b/solution.py
@@ -298,20 +298,19 @@
     data_ref, migration_ref, own_send, own_stage, own_recv, quarters_ref, ref_send, ref_stage, ref_recv,
     gains_ref, gain_ref, depth_ref, samples_ref, image_ref, total_ref, volume_ref,
     local_sems, quarter_sems, own_line, own_plane, ref_line, ref_plane_send, ref_plane_recv,
-    pair_send, pair_recv, to_next_sems, to_previous_sems,
+    to_next_sems, to_previous_sems,
 ):
     frame = lax.axis_index("frame")
     slab = lax.axis_index("slab")
     column, depth_place = slab // LINE, slab % LINE
     columns = slabs // LINE
     place_x, place_y, core = column // 2, column % 2, frame % 2
-    other_core = frame + 1 - 2 * core
     def distance(of_frame):
         return jnp.where(of_frame == 0, 1, jnp.where(of_frame == 1, 3, jnp.where(of_frame == 2, 0, 2)))
 
     frame_at = (2, 0, 3, 1)
     target_x = (place_x + distance(frame)) % RING
-    keeps = (target_x == place_x) & (core == place_y)
+    keeps = target_x == place_x
     has_next = slab < slabs - 1
     has_previous = slab > 0
     next_slab, previous_slab = (slab + 1) % slabs, (slab + slabs - 1) % slabs
@@ -350,12 +349,13 @@
     for i in range(1, columns):
         greet(on_plane(i))
     for i in range(RING):
-        x = (place_x + i) % RING
-        device = {"frame": frame_at[-i % RING], "slab": (x * 2 + core) * LINE + depth_place}
-        if i == 0:
-            pl.when(jnp.logical_not(keeps))(functools.partial(greet, device))
-        else:
-            greet(device)
+        for c in (1, 0):
+            from_column = (place_x + i) % RING * 2 + (place_y + c) % 2
+            device = {"frame": frame_at[-i % RING], "slab": from_column * LINE + depth_place}
+            if i == 0 and c == 0:
+                pl.when(jnp.logical_not(keeps))(functools.partial(greet, device))
+            else:
+                greet(device)
     for i in range(1, frames):
         greet({"frame": (frame + i) % frames, "slab": slab})
     pl.when(has_next)(lambda: greet({"frame": frame, "slab": next_slab}))
@@ -367,7 +367,7 @@
         copy.wait()
     gains_ref[1, :, :64] = gains_in_ref[...]
     pack_own(data_ref, own_send)
-    greetings = (LINE - 1) + (columns - 1) + 4 - jnp.where(keeps, 1, 0) + (frames - 1)
+    greetings = (LINE - 1) + (columns - 1) + 8 - jnp.where(keeps, 1, 0) + (frames - 1)
     greetings = greetings + jnp.where(has_next, 1, 0) + jnp.where(has_previous, 1, 0)
     pl.semaphore_wait(barrier, greetings)
 
@@ -416,9 +416,10 @@
     expand_gain(column_ref, gain_ref)
 
     wait_bytes(ref_stage, ref_line.at[1])
-    for a, b in ((1, 1), (1, 0), (0, 1), (0, 0)):
+    for i in range(7, -1, -1):
+        a, b, c = i // 4, i // 2 % 2, i % 2
         to_y = (place_y + a) % 2
-        to_frame = (frame // 2 + b) % 2 * 2 + place_y
+        to_frame = (frame // 2 + b) % 2 * 2 + (core + c) % 2
         copy = pltpu.make_async_remote_copy(
             src_ref=ref_stage.at[:, to_y],
             dst_ref=ref_recv.at[place_x, place_y],
@@ -427,7 +428,7 @@
             device_id={"frame": to_frame, "slab": (target_x * 2 + to_y) * LINE + depth_place},
             device_id_type=MESH,
         )
-        if a == 0 and b == 0:
+        if i == 0:
             pl.when(jnp.logical_not(keeps))(copy.start)
         else:
             copy.start()
@@ -444,20 +445,8 @@
     wait_bytes(own_recv, own_plane.at[1])
     unpack_own(own_recv, samples_ref)
     make_image(migration_ref, samples_ref, gain_ref, depth_ref, image_ref)
-    pieces = [(place_x + i) % RING for i in (0, 1, 3, 2)]
-    for x in pieces:
-        copy = pltpu.make_async_remote_copy(
-            src_ref=ref_recv.at[x, core],
-            dst_ref=ref_recv.at[x, core],
-            send_sem=pair_send.at[0],
-            recv_sem=pair_recv.at[x],
-            device_id={"frame": other_core, "slab": slab},
-            device_id_type=MESH,
-        )
-        wait_bytes(ref_recv.at[x, core], ref_plane_recv.at[x])
-        copy.start()
-    for x in pieces:
-        wait_bytes(ref_recv.at[x, 1 - core], pair_recv.at[x])
+    for x in range(RING):
+        wait_bytes(ref_recv.at[x], ref_plane_recv.at[x])
     reach = 2 * KX + 1
     reference_raw(migration_ref, ref_recv, total_ref, 0, reach * LY)
     reference_planes(total_ref, gain_ref, depth_ref, volume_ref, 0, reach)
@@ -485,15 +474,14 @@
     wait_bytes(ref_stage.at[pl.ds(0, LINE - 1)], ref_line.at[0])
     wait_bytes(own_recv.at[pl.ds(0, slabs - LINE)], own_plane.at[0])
 
-    wait_bytes(own_recv, pair_send.at[0])
 
     @pl.when(keeps)
     def _():
-        wait_bytes(own_recv.at[pl.ds(0, slabs // 4 * 3)], ref_plane_send.at[0])
+        wait_bytes(migration_ref.at[pl.ds(0, 112)], ref_plane_send.at[0])
 
     @pl.when(jnp.logical_not(keeps))
     def _():
-        wait_bytes(own_recv, ref_plane_send.at[0])
+        wait_bytes(ref_recv, ref_plane_send.at[0])
 
 
 def per_device(slabs, frames, element_data, migration, column_gain, depth_gain, coarse_shift, reference_frame):
@@ -537,8 +525,6 @@
             pltpu.SemaphoreType.DMA((2,)),
             pltpu.SemaphoreType.DMA((1,)),
             pltpu.SemaphoreType.DMA((RING,)),
-            pltpu.SemaphoreType.DMA((1,)),
-            pltpu.SemaphoreType.DMA((RING,)),
             pltpu.SemaphoreType.DMA((2,)),
             pltpu.SemaphoreType.DMA((2,)),
         ],

time: 30.3 us -> 30.2 us (level)
  no operation moved by 1% of the time
where the time goes in v9:
time: 30.2 us; the launch traced here: 30.1 us
  Pallas kernels  29.5 us (98%)
  between operations  0.66 us (2%)
    pallas_call x1, Pallas kernels, per_device(): pl.pallas_call(functools.partial(fused_kernel, slabs, frames), out_shape=...  28.2 us
    pallas_call x1, Pallas kernels, per_device(): pl.pallas_call(finish, out_shape=(jax.ShapeDtypeStruct((7, 4, 4, 8), f32)...  1.24 us

profile of v9, /device:TPU:1, one launch (start us, length us, event | category | flops | bytes accessed | tf_op | source)
XLA Modules:
  0.0 30.1 jit_solution(2612601578953953527)
XLA Ops:
  0.6 0.0 copy-start
  0.6 28.2 %shard_map.77.parts_ref = f32[4096,128]{1,0:T(8,128)S(1)} custom-call(s32[3,4,4,8]{3,2,1,0:T(4,128)} %bitcast.16, s32[4]{0:T(128)} %chosen_hbm.1, bf16[16,4096]{1,0:T(8,128)(2,1)} %bitcast.18, bf16[2048,1024]{1,0:T(8,128)(2,1)} %migration_hbm.1, f32[16,128]{1,0:T(8,128)} %bitcast.19, f32[1,64]{1,0:T(1,128)} %bitcast.20), custom_call_target="tpu_custom_call" | custom-call | tf_op jit(solution)/shard_map/pallas_call | solution.py:495
  28.9 0.0 copy-done
  28.9 1.2 %shard_map.78 = (f32[7,4,4,8]{3,2,1,0:T(4,128)}, f32[3,4,4,8]{3,2,1,0:T(4,128)}) custom-call(f32[4096,128]{1,0:T(8,128)S(1)} %shard_map.77.parts_ref, s32[3,4,4,8]{3,2,1,0:T(4,128)S(1)} %bitcast.17), custom_call_target="tpu_custom_call" | custom-call | tf_op jit(solution)/shard_map/pallas_call | solution.py:535
Async XLA Ops:
  0.6 28.3 %copy-start = (s32[3,1,4,8,4]{3,4,2,1,0:T(4,128)S(1)}, s32[3,1,4,8,4]{3,4,2,1,0:T(4,128)}, u32[]{:S(2)}) copy-start(s32[3,1,4,8,4]{3,4,2,1,0:T(4,128)} %param.10) | copy-start | bytes 4612
